TPU v7x, 256 devices: a whole 4x4x8 slice. The times are simulated.
256 devices in a mesh: tm: 64 (over y, x_hi, z), tp: 4 (over x_lo, core).
Axes of the slice: x: 4 (x_hi: 2, x_lo: 2; x = x_hi * 2 + x_lo), y: 4, z: 8, core: 2. Of those that a mesh axis runs over, the one named last changes fastest.
Arguments:
- queries: bfloat16 [32768, 2560], P('tm', 'tp'), may hold values from -24 to 24
- key_rows: bfloat16 [32768, 2560], P('tm', 'tp'), may hold values from -24 to 24
- value_rows: bfloat16 [32768, 2560], P('tm', 'tp'), may hold values from -6 to 6
- query_gain: float32 [2560], P('tp'), may hold values from 0.1 to 1.9
- key_gain: float32 [2560], P('tp'), may hold values from 0.1 to 1.9
- out_weight: bfloat16 [2560, 5120], P('tp'), may hold values from -0.5 to 0.5
- residual: bfloat16 [32768, 5120], P('tm', 'tp'), may hold values from -3 to 3
- gate_table: bfloat16 [50, 5120], P(None, 'tp'), may hold values from -8 to 8
- timesteps: int32 [64], P('tm'), may hold values from 0 to 49
- windows: int32 [64], P('tm'), may hold values from 1 to 4, as said below
- queue_positions: int32 [64], P('tm'), may hold values from 0 to 63, as said below
- fresh_span: bfloat16 [512, 5120], P(None, 'tp'), may hold values from -6 to 6
Outputs:
- advanced: bfloat16 [32768, 5120], P('tm', 'tp')
Inputs may be any that keep to these rules, and one draw needn't show every extreme that they name: `windows`: some span whose queue position is at most 59 has the value 4. A rotation: queue_positions[c] = (c - s) mod 64 for one slot s.
All inputs are finite; a program needn't handle non-finite values.
Results may differ from a plain program's by a relative error of at most 0.015.
Values may be sent and summed in bfloat16 or wider, within the bound.
A program may use at most 128 MiB of HBM per device.

v0:
```python
import jax
import jax.numpy as jnp
from jax import lax
from jax.sharding import PartitionSpec as P

HD = 128
WMAX = 4


epsilon = 1e-06


def from_behind(value, axis, by):
    count = lax.axis_size(axis)
    return lax.ppermute(value, axis, [(i, (i + by) % count) for i in range(count)])


def local(
    queries,
    key_rows,
    value_rows,
    query_gain,
    key_gain,
    out_weight,
    residual,
    gate_table,
    timesteps,
    windows,
    queue_positions,
    fresh_span,
):
    spans = lax.axis_size("tm")
    rows, local_width = queries.shape
    width = local_width * lax.axis_size("tp")
    local_heads = local_width // HD
    query_wide = queries.astype(jnp.float32)
    key_wide = key_rows.astype(jnp.float32)
    query_energy, key_energy = lax.psum(
        (jnp.sum(query_wide * query_wide, axis=1), jnp.sum(key_wide * key_wide, axis=1)), "tp"
    )
    query_norm = (
        query_wide * lax.rsqrt(query_energy / width + epsilon)[:, None] * query_gain[None, :]
    ).astype(jnp.bfloat16)
    key_norm = (
        key_wide * lax.rsqrt(key_energy / width + epsilon)[:, None] * key_gain[None, :]
    ).astype(jnp.bfloat16)
    position = queue_positions[0]
    reach = windows[0]
    blocks = [(key_norm, value_rows, jnp.array(True))]
    for distance in range(1, WMAX + 1):
        older_keys, older_values = from_behind((key_norm, value_rows), "tm", -distance)
        allowed = jnp.logical_and(distance <= reach, position + distance <= spans - 1)
        blocks.append((older_keys, older_values, allowed))
    query_heads = query_norm.reshape(rows, local_heads, HD)
    factor_scale = HD ** (-0.5)

    def block_scores(block):
        key_heads = block[0].reshape(rows, local_heads, HD)
        scores = (
            jnp.einsum("qhd,khd->hqk", query_heads, key_heads, preferred_element_type=jnp.float32)
            * factor_scale
        )
        return jnp.where(block[2], scores, -jnp.inf)

    def block_values(block):
        return block[1].reshape(rows, local_heads, HD)

    scores = jnp.concatenate([block_scores(block) for block in blocks], axis=2)
    values_all = jnp.concatenate([block_values(block) for block in blocks], axis=0)
    peak = jnp.max(scores, axis=2, keepdims=True)
    expo = jnp.exp(scores - peak)
    total = jnp.sum(expo, axis=2, keepdims=True)
    mixed = (
        jnp.einsum(
            "hqk,khd->hqd",
            expo.astype(jnp.bfloat16),
            values_all,
            preferred_element_type=jnp.float32,
        )
        / total
    )
    attended = jnp.transpose(mixed, (1, 0, 2)).reshape(rows, local_width).astype(jnp.bfloat16)
    partial_value = jnp.dot(attended, out_weight, preferred_element_type=jnp.float32)
    projected = lax.psum_scatter(
        partial_value.astype(jnp.bfloat16), "tp", scatter_dimension=1, tiled=True
    ).astype(jnp.float32)
    gate = lax.dynamic_index_in_dim(gate_table, timesteps[0], 0, keepdims=False).astype(jnp.float32)
    updated = (residual.astype(jnp.float32) + gate[None, :] * projected).astype(jnp.bfloat16)
    moved = from_behind(updated, "tm", 1)
    return jnp.where(position == 0, fresh_span, moved)


def solution(mesh):
    placed = (
        P("tm", "tp"),
        P("tm", "tp"),
        P("tm", "tp"),
        P("tp"),
        P("tp"),
        P("tp", None),
        P("tm", "tp"),
        P(None, "tp"),
        P("tm"),
        P("tm"),
        P("tm"),
        P(None, "tp"),
    )
    return jax.shard_map(
        local, mesh=mesh, in_specs=placed, out_specs=P("tm", "tp"), check_vma=False
    )
```

profile of v0, /device:TPU:1, one launch (start us, length us, event | category | flops | bytes accessed | tf_op | source)
XLA Modules:
  0.0 388.0 jit_solution(15401175740221048580)
XLA Ops:
  6.5 0.0 copy-start.4
  6.5 0.0 reduce-scatter.2.cloned.1.call-start
  6.5 1.3 copy.25
  7.9 0.0 copy-start.1
  7.9 1.6 copy.26
  9.5 0.3 fusion.16
  9.8 8.3 %all-reduce = (f32[512]{0:T(512)S(1)}, f32[512]{0:T(512)S(1)}) all-reduce(f32[512]{0:T(512)S(1)} %get-tuple-element.17, f32[512]{0:T(512)S(1)} %get-tuple-element.18), channel_id=1, replica_groups=mesh['tm'=64,'tp'=4] {'tp'}, use_global_device_ids=true, to_apply=%region_1.0 | all-reduce | flops 1024 | bytes 8192 | tf_op jit(solution)/shard_map/psum | solution.py:38
  18.0 1.7 fusion.21
  19.7 8.8 %collective-permute-start = (bf16[512,640]{0,1:T(8,128)(2,1)}, bf16[512,640]{0,1:T(8,128)(2,1)}, u32[]{:S(2)}, u32[]{:S(2)}) collective-permute-start(bf16[512,640]{0,1:T(8,128)(2,1)} %fusion.21), channel_id=1, source_target_pairs={{0,252},{4,0},{8,4},{12,8},{16,12},{20,16},{24,20},{28,24},{32,28}... | collective-permute-start | bytes 1966088 | tf_op jit(solution)/shard_map/ppermute | solution.py:15
  28.5 1.2 collective-permute-start.1
  29.7 0.4 collective-permute-start.2
  30.1 4.4 %collective-permute-start.3 = (bf16[512,640]{0,1:T(8,128)(2,1)}, bf16[512,640]{0,1:T(8,128)(2,1)}, u32[]{:S(2)}, u32[]{:S(2)}) collective-permute-start(bf16[512,640]{0,1:T(8,128)(2,1)} %fusion.21), channel_id=1, source_target_pairs={{0,240},{4,244},{8,248},{12,252},{16,0},{20,4},{24,8},{28,12},{32,... | collective-permute-start | bytes 1966088 | tf_op jit(solution)/shard_map/ppermute | solution.py:15
  34.5 0.7 collective-permute-start.4
  35.2 2.2 copy.37
  37.4 0.0 copy-done.1
  37.4 1.1 constant_dynamic-update-slice_fusion.4
  39.9 0.0 copy-done.4
  39.9 1.3 fusion.18
  41.2 2.0 multiply_reduce_fusion
  43.2 10.6 %collective-permute-done = bf16[512,640]{0,1:T(8,128)(2,1)} collective-permute-done((bf16[512,640]{0,1:T(8,128)(2,1)}, bf16[512,640]{0,1:T(8,128)(2,1)}, u32[]{:S(2)}, u32[]{:S(2)}) %collective-permute-start) | collective-permute-done | bytes 655392 | tf_op jit(solution)/shard_map/ppermute | solution.py:15
  53.8 0.0 collective-permute-start.5
  53.8 2.0 fusion.5
  55.8 27.0 %collective-permute-done.1 = bf16[512,640]{0,1:T(8,128)(2,1)} collective-permute-done((bf16[512,640]{0,1:T(8,128)(2,1)}, bf16[512,640]{0,1:T(8,128)(2,1)}, u32[]{:S(2)}, u32[]{:S(2)}) %collective-permute-start.1) | collective-permute-done | bytes 655392 | tf_op jit(solution)/shard_map/ppermute | solution.py:15
  82.8 0.0 collective-permute-start.6
  82.8 2.0 fusion.7
  84.8 54.9 %collective-permute-done.2 = bf16[512,640]{0,1:T(8,128)(2,1)} collective-permute-done((bf16[512,640]{0,1:T(8,128)(2,1)}, bf16[512,640]{0,1:T(8,128)(2,1)}, u32[]{:S(2)}, u32[]{:S(2)}) %collective-permute-start.2) | collective-permute-done | bytes 655392 | tf_op jit(solution)/shard_map/ppermute | solution.py:15
  139.6 0.0 collective-permute-start.7
  139.6 2.0 fusion.9
  141.6 0.0 collective-permute-done.3
  141.6 2.0 fusion.11
  143.6 0.0 copy-start
  143.6 3.8 fusion
  147.5 5.0 %copy-done = f32[5,512,2560]{1,2,0:T(8,128)} copy-done((f32[5,512,2560]{1,2,0:T(8,128)}, f32[5,512,2560]{1,2,0:T(8,128)S(1)}, u32[]{:S(2)}) %copy-start) | copy-done | bytes 26214424
  152.5 13.7 %collective-permute-done.4 = bf16[512,640]{1,0:T(8,128)(2,1)} collective-permute-done((bf16[512,640]{1,0:T(8,128)(2,1)}, bf16[512,640]{1,0:T(8,128)(2,1)}, u32[]{:S(2)}, u32[]{:S(2)}) %collective-permute-start.4) | collective-permute-done | bytes 655392 | tf_op jit(solution)/shard_map/ppermute | solution.py:15
  166.2 2.2 copy.38
  168.4 27.1 %collective-permute-done.5 = bf16[512,640]{1,0:T(8,128)(2,1)} collective-permute-done((bf16[512,640]{1,0:T(8,128)(2,1)}, bf16[512,640]{1,0:T(8,128)(2,1)}, u32[]{:S(2)}, u32[]{:S(2)}) %collective-permute-start.5) | collective-permute-done | bytes 655392 | tf_op jit(solution)/shard_map/ppermute | solution.py:15
  195.4 2.2 copy.39
  197.6 54.4 %collective-permute-done.6 = bf16[512,640]{1,0:T(8,128)(2,1)} collective-permute-done((bf16[512,640]{1,0:T(8,128)(2,1)}, bf16[512,640]{1,0:T(8,128)(2,1)}, u32[]{:S(2)}, u32[]{:S(2)}) %collective-permute-start.6) | collective-permute-done | bytes 655392 | tf_op jit(solution)/shard_map/ppermute | solution.py:15
  252.0 2.2 copy.40
  254.2 1.1 constant_dynamic-update-slice_fusion.3
  255.3 1.1 constant_dynamic-update-slice_fusion.2
  256.4 1.1 constant_dynamic-update-slice_fusion.1
  257.6 0.0 collective-permute-done.7
  257.6 2.2 copy.41
  259.8 1.1 constant_dynamic-update-slice_fusion
  260.9 13.0 %divide_convert_fusion = bf16[512,5,128]{0,2,1:T(8,128)(2,1)S(1)} fusion(bf16[2560,5,128]{0,2,1:T(8,128)(2,1)S(1)} %constant_dynamic-update-slice_fusion, f32[5,512,2560]{1,2,0:T(8,128)} %copy-done, f32[5,512]{1,0:T(8,128)S(1)} %maximum_maximum_fusion, f32[512,5]{0,1:T(8,128)S(1)} %bitcast.50), kind=kOutput, calls=%fused_computation.32 | convolution fusion | flops 1691484160 | bytes 30167040 | tf_op jit(solution)/shard_map/hqk,khd->hqd/dot_general | solution.py:74
  273.9 8.9 %convolution_convert_fusion = bf16[512,5120]{1,0:T(8,128)(2,1)} fusion(bf16[512,640]{0,1:T(8,128)(2,1)S(1)} %bitcast.49, bf16[640,5120]{1,0:T(8,128)(2,1)} %param.17), kind=kOutput, calls=%fused_computation.5 | convolution fusion | flops 3358064640 | bytes 12451840 | tf_op jit(solution)/shard_map/dot_general | solution.py:83
  282.8 0.0 copy-start.3
  282.8 0.0 copy-start.2
  282.8 0.0 reduce-scatter.2.cloned.1.call-update
  283.6 0.8 convert_reduce_fusion
  284.4 57.8 %reduce-scatter.2.cloned.1.call-done = bf16[512,1280]{1,0:T(8,128)(2,1)} async-done(((bf16[512,5120]{1,0:T(8,128)(2,1)}), bf16[512,1280]{1,0:T(8,128)(2,1)}) %reduce-scatter.2.cloned.1.call-update) | async-done | bytes 1310736 | tf_op jit(solution)/shard_map/reduce_scatter | solution.py:84
  342.2 0.0 copy-done.3
  342.2 1.7 add_convert_fusion
  343.9 1.3 collective-permute-start.8
  345.3 34.7 %collective-permute-done.8 = bf16[512,1280]{1,0:T(8,128)(2,1)S(1)} collective-permute-done((bf16[512,1280]{1,0:T(8,128)(2,1)S(1)}, bf16[512,1280]{1,0:T(8,128)(2,1)S(1)}, u32[]{:S(2)}, u32[]{:S(2)}) %collective-permute-start.8) | collective-permute-done | bytes 1310752 | tf_op jit(solution)/shard_map/ppermute | solution.py:15
  380.0 0.0 copy-done.2
  380.0 1.2 broadcast_select_fusion
  (3 shorter events, 0.0 us)
Async XLA Ops:
  6.5 33.4 %copy-start.4 = (f32[640]{0:T(1024)S(1)}, f32[640]{0:T(1024)}, u32[]{:S(2)}) copy-start(f32[640]{0:T(1024)} %param.15) | copy-start | bytes 7684
  6.5 335.7 %reduce-scatter.2.cloned.1.call-start = ((), (), s32[]{:S(2)}) async-start(), calls=%async_computation.1 | async-start | bytes 6553600 | tf_op jit(solution)/shard_map/reduce_scatter | solution.py:84
  7.9 29.6 %copy-start.1 = (bf16[512,640]{0,1:T(8,128)(2,1)}, bf16[512,640]{0,1:T(8,128)(2,1)S(1)}, u32[]{:S(2)}) copy-start(bf16[512,640]{0,1:T(8,128)(2,1)S(1)} %copy.25) | copy-start | bytes 1966084
  19.7 34.1 %collective-permute-start = (bf16[512,640]{0,1:T(8,128)(2,1)}, bf16[512,640]{0,1:T(8,128)(2,1)}, u32[]{:S(2)}, u32[]{:S(2)}) collective-permute-start(bf16[512,640]{0,1:T(8,128)(2,1)} %fusion.21), channel_id=1, source_target_pairs={{0,252},{4,0},{8,4},{12,8},{16,12},{20,16},{24,20},{28,24},{32,28}... | collective-permute-start | bytes 1966088 | tf_op jit(solution)/shard_map/ppermute | solution.py:15
  28.5 54.3 %collective-permute-start.1 = (bf16[512,640]{0,1:T(8,128)(2,1)}, bf16[512,640]{0,1:T(8,128)(2,1)}, u32[]{:S(2)}, u32[]{:S(2)}) collective-permute-start(bf16[512,640]{0,1:T(8,128)(2,1)} %fusion.21), channel_id=1, source_target_pairs={{0,248},{4,252},{8,0},{12,4},{16,8},{20,12},{24,16},{28,20},{32,24... | collective-permute-start | bytes 1966088 | tf_op jit(solution)/shard_map/ppermute | solution.py:15
  29.7 110.0 %collective-permute-start.2 = (bf16[512,640]{0,1:T(8,128)(2,1)}, bf16[512,640]{0,1:T(8,128)(2,1)}, u32[]{:S(2)}, u32[]{:S(2)}) collective-permute-start(bf16[512,640]{0,1:T(8,128)(2,1)} %fusion.21), channel_id=1, source_target_pairs={{0,244},{4,248},{8,252},{12,0},{16,4},{20,8},{24,12},{28,16},{32,2... | collective-permute-start | bytes 1966088 | tf_op jit(solution)/shard_map/ppermute | solution.py:15
  30.1 111.5 %collective-permute-start.3 = (bf16[512,640]{0,1:T(8,128)(2,1)}, bf16[512,640]{0,1:T(8,128)(2,1)}, u32[]{:S(2)}, u32[]{:S(2)}) collective-permute-start(bf16[512,640]{0,1:T(8,128)(2,1)} %fusion.21), channel_id=1, source_target_pairs={{0,240},{4,244},{8,248},{12,252},{16,0},{20,4},{24,8},{28,12},{32,... | collective-permute-start | bytes 1966088 | tf_op jit(solution)/shard_map/ppermute | solution.py:15
  34.5 131.7 %collective-permute-start.4 = (bf16[512,640]{1,0:T(8,128)(2,1)}, bf16[512,640]{1,0:T(8,128)(2,1)}, u32[]{:S(2)}, u32[]{:S(2)}) collective-permute-start(bf16[512,640]{1,0:T(8,128)(2,1)} %param.14), channel_id=1, source_target_pairs={{0,252},{4,0},{8,4},{12,8},{16,12},{20,16},{24,20},{28,24},{32,28}... | collective-permute-start | bytes 1966088 | tf_op jit(solution)/shard_map/ppermute | solution.py:15
  53.8 141.6 %collective-permute-start.5 = (bf16[512,640]{1,0:T(8,128)(2,1)}, bf16[512,640]{1,0:T(8,128)(2,1)}, u32[]{:S(2)}, u32[]{:S(2)}) collective-permute-start(bf16[512,640]{1,0:T(8,128)(2,1)} %param.14), channel_id=1, source_target_pairs={{0,248},{4,252},{8,0},{12,4},{16,8},{20,12},{24,16},{28,20},{32,24... | collective-permute-start | bytes 1966088 | tf_op jit(solution)/shard_map/ppermute | solution.py:15
  82.8 169.2 %collective-permute-start.6 = (bf16[512,640]{1,0:T(8,128)(2,1)}, bf16[512,640]{1,0:T(8,128)(2,1)}, u32[]{:S(2)}, u32[]{:S(2)}) collective-permute-start(bf16[512,640]{1,0:T(8,128)(2,1)} %param.14), channel_id=1, source_target_pairs={{0,244},{4,248},{8,252},{12,0},{16,4},{20,8},{24,12},{28,16},{32,2... | collective-permute-start | bytes 1966088 | tf_op jit(solution)/shard_map/ppermute | solution.py:15
  139.6 118.0 %collective-permute-start.7 = (bf16[512,640]{1,0:T(8,128)(2,1)}, bf16[512,640]{1,0:T(8,128)(2,1)}, u32[]{:S(2)}, u32[]{:S(2)}) collective-permute-start(bf16[512,640]{1,0:T(8,128)(2,1)} %param.14), channel_id=1, source_target_pairs={{0,240},{4,244},{8,248},{12,252},{16,0},{20,4},{24,8},{28,12},{32,... | collective-permute-start | bytes 1966088 | tf_op jit(solution)/shard_map/ppermute | solution.py:15
  143.6 8.8 %copy-start = (f32[5,512,2560]{1,2,0:T(8,128)}, f32[5,512,2560]{1,2,0:T(8,128)S(1)}, u32[]{:S(2)}) copy-start(f32[5,512,2560]{1,2,0:T(8,128)S(1)} %get-tuple-element.16) | copy-start | bytes 78643200
  282.8 59.4 %copy-start.3 = (bf16[512,1280]{1,0:T(8,128)(2,1)S(1)}, bf16[512,1280]{1,0:T(8,128)(2,1)}, u32[]{:S(2)}) copy-start(bf16[512,1280]{1,0:T(8,128)(2,1)} %param.18) | copy-start | bytes 3932164
  282.8 97.2 %copy-start.2 = (bf16[512,1280]{1,0:T(8,128)(2,1)S(1)}, bf16[512,1280]{1,0:T(8,128)(2,1)}, u32[]{:S(2)}) copy-start(bf16[512,1280]{1,0:T(8,128)(2,1)} %param.23) | copy-start | bytes 3932164
  343.9 36.1 %collective-permute-start.8 = (bf16[512,1280]{1,0:T(8,128)(2,1)S(1)}, bf16[512,1280]{1,0:T(8,128)(2,1)S(1)}, u32[]{:S(2)}, u32[]{:S(2)}) collective-permute-start(bf16[512,1280]{1,0:T(8,128)(2,1)S(1)} %add_convert_fusion), channel_id=1, source_target_pairs={{0,4},{4,8},{8,12},{12,16},{16,20},{20,24},{24,28},{28,32},{32,36}... | collective-permute-start | bytes 3932168 | tf_op jit(solution)/shard_map/ppermute | solution.py:15
Sparse Core Ops, SparseCore 0:
  283.0 59.2 reduce-scatter.1
where the time goes:
time: 389 us; the launch traced here: 388 us
  waiting for transfers between devices  280 us (72%)
  matrix products  31.8 us (8%)
  local copies, waits for them, and re-layouts  24.5 us (6%)
  starting transfers between devices  16.9 us (4%)
  between operations  15.7 us (4%)
  other arithmetic  10.7 us (3%)
  blocking collectives  8.25 us (2%)
    ppermute x9, waiting for transfers between devices, from_behind(): lax.ppermute(value, axis, [(i, (i + by) % count) for i in range(count)])  222 us
    reduce_scatter x1, waiting for transfers between devices, local(): lax.psum_scatter(partial_value.astype(jnp.bfloat16), 'tp', scatter_dimens...  57.8 us
    ppermute x9, starting transfers between devices, from_behind(): lax.ppermute(value, axis, [(i, (i + by) % count) for i in range(count)])  16.9 us
    unnamed x17, local copies, waits for them, and re-layouts  14.7 us
    dot_general x1, matrix products, local(): jnp.einsum('hqk,khd->hqd', expo.astype(jnp.bfloat16), values_all, preferr...  13 us
    dot_general x5, matrix products, block_scores(): jnp.einsum('qhd,khd->hqk', query_heads, key_heads, preferred_element_type...  9.92 us
    dot_general x1, matrix products, local(): jnp.dot(attended, out_weight, preferred_element_type=jnp.float32)  8.92 us
    ppermute x4, local copies, waits for them, and re-layouts, from_behind(): lax.ppermute(value, axis, [(i, (i + by) % count) for i in range(count)])  8.67 us
  transfers between devices with their start and end apart: 10, of which 8 were waited for; matrix products, arithmetic and copies ran while one was open for 7% of the time, Pallas kernels for 0%

commit v1 on v0

v1 whole, which is shorter than its diff:
```python
import jax
import jax.numpy as jnp
from jax import lax
from jax.experimental import pallas as pl
from jax.experimental.pallas import tpu as pltpu
from jax.sharding import PartitionSpec as P

HD = 128
WMAX = 4
EPS = 1e-06
FEW = -1e30
MANY = 1e30
LOG2E = 1.4426950408889634
MESH = pl.DeviceIdType.MESH
F32 = jnp.float32
BF16 = jnp.bfloat16


def kernel(
    spans,
    q_hbm,
    k_hbm,
    v_hbm,
    gain_ref,
    w_hbm,
    res_hbm,
    gate_ref,
    step_ref,
    reach_ref,
    pos_ref,
    out_ref,
    q_own,
    k_own,
    v_own,
    vt_own,
    qn,
    kn,
    qa,
    qb,
    k1,
    vt1,
    k2,
    vt2,
    est,
    st_own,
    st_in,
    os_out,
    os_stat,
    os_in,
    os_in_stat,
    far_out,
    far_stat,
    far_in,
    far_in_stat,
    acc,
    top,
    ag,
    wbuf,
    res,
    total,
    load_sem,
    wload_sem,
    est_s,
    est_r,
    st_s,
    st_r,
    q_s,
    q_r,
    qf_s,
    qf_r,
    k_s,
    k_r,
    v_s,
    v_r,
    kf_s,
    kf_r,
    vf_s,
    vf_r,
    os_s,
    os_r,
    oss_s,
    oss_r,
    far_s,
    far_r,
    fars_s,
    fars_r,
    res_s,
    res_r,
    wsib_s,
    wsib_r,
    wx_s,
    wx_r,
    wy_s,
    wy_r,
    ag_s,
    ag_r,
):
    heads, rows = q_own.shape[0], q_own.shape[1]
    local = heads * HD
    width = 4 * local
    out_cols = out_ref.shape[1]
    half_cols = out_cols // 2
    tm = lax.axis_index("tm")
    tp = lax.axis_index("tp")
    lo, core = tp // 2, tp % 2
    x_hi, y, z = (tm // 8) % 2, tm // 16, tm % 8

    def shifted(by):
        return (lax.rem(tm + by + spans, spans), tp)

    peers = [(tm, lax.rem(tp + by, 4)) for by in (1, 2, 3)]
    across = [(tm + 8 - 16 * x_hi, (1 - lo) * 2 + c) for c in (0, 1)]
    turn = jnp.where(z >= 4, -16, 16)
    y_next, y_prev = shifted(turn), shifted(-turn)
    turn_y = turn // 16

    def load(src, dst, slot, h):
        return pltpu.make_async_copy(
            src.at[:, pl.ds(pl.multiple_of(h * HD, HD), HD)], dst.at[h], load_sem.at[slot, h]
        )

    loads = [(q_hbm, q_own, 0), (k_hbm, k_own, 1), (v_hbm, v_own, 2)]
    for src, dst, slot in loads:
        for h in range(heads):
            load(src, dst, slot, h).start()

    barrier = pltpu.get_barrier_semaphore()
    greet = [shifted(1), shifted(-1), shifted(2), shifted(-2)] + peers + across + [y_prev]
    for other in greet:
        pl.semaphore_signal(barrier, inc=1, device_id=other, device_id_type=MESH)

    w_own_copy = pltpu.make_async_copy(
        w_hbm.at[:, :, pl.ds(pl.multiple_of(tp * out_cols, HD), out_cols)],
        wbuf.at[:, pl.ds(pl.multiple_of(tp * HD, HD), HD), :],
        wload_sem,
    )
    w_own_copy.start()

    ones = jnp.ones((16, rows), BF16)
    for h in range(heads):
        vt_own[h, HD : HD + 16, :] = ones
        vt1[h, HD : HD + 16, :] = ones
        vt2[h, HD : HD + 16, :] = ones

    def energy_of(ref, slot, src):
        squares = jnp.zeros((rows, HD), F32)
        for h in range(heads):
            load(src, ref, slot, h).wait()
            wide = ref[h].astype(F32)
            squares = squares + wide * wide
        return jnp.sum(jnp.transpose(squares), axis=0, keepdims=True)

    energy_q = energy_of(q_own, 0, q_hbm)
    energy_k = energy_of(k_own, 1, k_hbm)
    line = lax.broadcasted_iota(jnp.int32, (8, rows), 0)
    message = jnp.where(line == 0, energy_q, 0.0)
    message = jnp.where(line == 1, energy_k, message)
    message = jnp.where(line == 2, reach_ref[0].astype(F32) * 0.25, message)
    message = jnp.where(line == 3, step_ref[0].astype(F32) * 0.25, message)
    est[tp] = message

    for h in range(heads):
        load(v_hbm, v_own, 2, h).wait()
        vt_own[h, :HD, :] = jnp.transpose(v_own[h])

    pl.semaphore_wait(barrier, len(greet))

    def remote(src, dst, send, recv, to):
        return pltpu.make_async_remote_copy(
            src_ref=src, dst_ref=dst, send_sem=send, recv_sem=recv, device_id=to, device_id_type=MESH
        )

    up, down = shifted(1), shifted(-1)
    est_copies = [
        remote(est.at[tp], est.at[tp], est_s.at[i], est_r.at[tp], to) for i, to in enumerate(peers)
    ]

    def est_in(i):
        who = lax.rem(tp + i + 1, 4)
        return remote(est.at[who], est.at[who], est_s.at[i], est_r.at[who], peers[i])

    def q_copy(h):
        return remote(q_own.at[h], qa.at[h], q_s.at[h], q_r.at[h], up)

    def q_forward(h):
        return remote(qa.at[h], qb.at[h], qf_s.at[h], qf_r.at[h], up)

    def k_copy(h):
        return remote(k_own.at[h], k1.at[h], k_s.at[h], k_r.at[h], down)

    def v_copy(h):
        return remote(
            vt_own.at[h, pl.ds(0, HD), :], vt1.at[h, pl.ds(0, HD), :], v_s.at[h], v_r.at[h], down
        )

    def k_forward(h):
        return remote(k1.at[h], k2.at[h], kf_s.at[h], kf_r.at[h], down)

    def v_forward(h):
        return remote(
            vt1.at[h, pl.ds(0, HD), :], vt2.at[h, pl.ds(0, HD), :], vf_s.at[h], vf_r.at[h], down
        )

    def os_copy(h):
        return remote(os_out.at[h], os_in.at[h], os_s.at[h], os_r.at[h], up)

    def os_stat_copy(h):
        return remote(os_stat.at[h], os_in_stat.at[h], oss_s.at[h], oss_r.at[h], up)

    def far_copy(h):
        return remote(far_out.at[h], far_in.at[h], far_s.at[h], far_r.at[h], down)

    def far_stat_copy(h):
        return remote(far_stat.at[h], far_in_stat.at[h], fars_s.at[h], fars_r.at[h], down)

    parts = res_s.shape[0]
    part_rows = rows // parts

    def res_copy(i):
        cut = pl.ds(i * part_rows, part_rows)
        return remote(res_hbm.at[cut], res.at[cut], res_s.at[i], res_r.at[i], up)

    def st_copy(i, by):
        return remote(st_own, st_in.at[i], st_s.at[i], st_r.at[i], shifted(by))

    sibling = (tm, lo * 2 + 1 - core)

    def w_slot(h, who, half):
        return wbuf.at[
            h,
            pl.ds(pl.multiple_of(who * HD, HD), HD),
            pl.ds(pl.multiple_of(half * half_cols, HD), half_cols),
        ]

    def w_sibling():
        return remote(
            w_hbm.at[:, :, pl.ds(pl.multiple_of(sibling[1] * out_cols, HD), out_cols)],
            wbuf.at[:, pl.ds(pl.multiple_of(tp * HD, HD), HD), :],
            wsib_s,
            wsib_r,
            sibling,
        )

    def w_across(c, h):
        column = across[c][1] * out_cols + lax.rem(y, 2) * half_cols
        return remote(
            w_hbm.at[h, :, pl.ds(pl.multiple_of(column, HD), half_cols)],
            w_slot(h, tp, lax.rem(y, 2)),
            wx_s.at[c, h],
            wx_r.at[h],
            across[c],
        )

    def w_piece(piece, h):
        return w_slot(h, (1 - lo) * 2 + piece // 2, lax.rem(piece, 2))

    def w_across_in(h):
        slot = w_piece(y, h)
        return remote(slot, slot, wx_s.at[0, h], wx_r.at[h], across[0])

    def w_along(k, h):
        slot = w_piece(lax.rem(y - turn_y * k + 4, 4), h)
        return remote(slot, slot, wy_s.at[k, h], wy_r.at[k, h], y_next)

    def w_along_in(k, h):
        slot = w_piece(lax.rem(y - turn_y * (k + 1) + 8, 4), h)
        return remote(slot, slot, wy_s.at[k, h], wy_r.at[k, h], y_next)

    def ag_slot(h, who):
        return ag.at[h, :, pl.ds(pl.multiple_of(who * HD, HD), HD)]

    def ag_copy(i, h):
        return remote(ag_slot(h, tp), ag_slot(h, tp), ag_s.at[i, h], ag_r.at[tp, h], peers[i])

    def ag_in(i, h):
        who = lax.rem(tp + i + 1, 4)
        return remote(ag_slot(h, who), ag_slot(h, who), ag_s.at[i, h], ag_r.at[who, h], peers[i])

    def each(body):
        @pl.loop(0, heads)
        def _(h):
            body(h)

    for copy in est_copies:
        copy.start()
    for h in range(2):
        q_copy(h).start()
        k_copy(h).start()
        v_copy(h).start()

    for i in range(3):
        est_in(i).wait_recv()
    st_own[...] = est[0] + est[1] + est[2] + est[3]
    st_moves = [(0, 1), (1, 2), (2, -1), (3, -2)]
    for i, by in st_moves:
        st_copy(i, by).start()

    @pl.loop(2, heads)
    def _(h):
        q_copy(h).start()
        k_copy(h).start()
        v_copy(h).start()

    @pl.when(core == y // 2)
    def _():
        @pl.loop(0, heads)
        def _(h):
            w_across(0, h).start()
            w_across(1, h).start()

    w_sibling().start()

    def column(state, row):
        scale = lax.rsqrt(state[row : row + 1, :] / width + EPS)
        return jnp.transpose(jnp.broadcast_to(scale, (HD, rows)))

    def unit_q(raw, scale, h):
        return (raw.astype(F32) * scale * gain_ref[pl.ds(h, 1), :]).astype(BF16)

    def unit_k(raw, scale):
        return (raw.astype(F32) * scale).astype(BF16)

    def scores_of(keys, queries):
        return lax.dot_general(
            keys, queries, (((1,), (1,)), ((), ())), preferred_element_type=F32
        )

    def alone(keys, queries, values):
        scores = scores_of(keys, queries)
        peak = jnp.max(scores, axis=0, keepdims=True)
        weight = jnp.exp2(scores - peak).astype(BF16)
        return jnp.dot(values, weight, preferred_element_type=F32), peak

    line_8 = lax.broadcasted_iota(jnp.int32, (8, rows), 0)

    def pair(first, second):
        return jnp.where(line_8 == 0, first, second)

    q_scale = column(st_own, 0)
    k_scale = column(st_own, 1)

    def self_part(h):
        q_copy(h).wait_recv()
        q_forward(h).start()
        kn[h] = unit_k(k_own[h], k_scale)
        mixed, peak = alone(kn[h], unit_q(q_own[h], q_scale, h), vt_own[h])
        os_out[h] = mixed[:HD].astype(BF16)
        os_stat[h] = pair(peak, mixed[HD : HD + 1])
        os_copy(h).start()
        os_stat_copy(h).start()

    each(self_part)
    for i in range(parts):
        res_copy(i).start()

    st_copy(0, 1).wait_recv()
    state_a = st_in.at[0]
    reach = state_a[2:3, :]
    step = state_a[3:4, :1]
    place = lax.rem(pos_ref[0] + spans - 1, spans)

    def live(distance):
        inside = (place + distance <= spans - 1).astype(F32)
        return jnp.logical_and(reach >= distance, inside > 0.5)

    qa_scale = column(state_a, 0)

    def near_part(h):
        qn[h] = unit_q(qa[h], qa_scale, h)
        scores = scores_of(kn[h], qn[h])
        allowed = live(1)
        peak = jnp.max(scores, axis=0, keepdims=True)
        weight = jnp.exp2(scores - jnp.where(allowed, peak, MANY)).astype(BF16)
        acc[h] = jnp.dot(vt_own[h], weight, preferred_element_type=F32)
        top[h] = jnp.broadcast_to(jnp.where(allowed, peak, FEW), (8, rows))

    each(near_part)

    def join(h, keys, values, allowed):
        scores = scores_of(keys, qn[h])
        before = top[h][:1]
        peak = jnp.where(allowed, jnp.max(scores, axis=0, keepdims=True), FEW)
        after = jnp.maximum(before, peak)
        weight = jnp.exp2(scores - jnp.where(allowed, after, MANY)).astype(BF16)
        acc[h] = acc[h] * jnp.exp2(before - after) + jnp.dot(
            values, weight, preferred_element_type=F32
        )
        top[h] = jnp.broadcast_to(after, (8, rows))

    st_copy(2, -1).wait_recv()
    k1_scale = column(st_in.at[2], 1)

    def second_part(h):
        k_copy(h).wait_recv()
        k_forward(h).start()
        v_copy(h).wait_recv()
        v_forward(h).start()
        join(h, unit_k(k1[h], k1_scale), vt1[h], live(2))
        w_across_in(h).wait_recv()
        w_along(0, h).start()

    each(second_part)

    st_copy(1, 2).wait_recv()
    st_copy(3, -2).wait_recv()
    qb_scale = column(st_in.at[1], 0)
    k2_scale = column(st_in.at[3], 1)

    def third_part(h):
        q_forward(h).wait_recv()
        k_forward(h).wait_recv()
        v_forward(h).wait_recv()
        keys = unit_k(k2[h], k2_scale)
        mixed, peak = alone(keys, unit_q(qb[h], qb_scale, h), vt2[h])
        far_out[h] = mixed[:HD].astype(BF16)
        far_stat[h] = pair(peak, mixed[HD : HD + 1])
        far_copy(h).start()
        far_stat_copy(h).start()
        join(h, keys, vt2[h], live(3))
        w_along_in(0, h).wait_recv()
        w_along(1, h).start()

    each(third_part)

    def project(h):
        for i in range(3):
            ag_in(i, h).wait_recv()
        w_along_in(2, h).wait_recv()

        @pl.loop(0, out_cols // 256)
        def _(j):
            cut = pl.ds(pl.multiple_of(j * 256, 256), 256)
            fresh = jnp.dot(ag[h], wbuf[h, :, cut], preferred_element_type=F32)
            total[:, cut] = total[:, cut] + fresh

    total[...] = jnp.zeros_like(total)

    def merge(h):
        w_along_in(1, h).wait_recv()
        w_along(2, h).start()
        os_copy(h).wait_recv()
        os_stat_copy(h).wait_recv()
        far_copy(h).wait_recv()
        far_stat_copy(h).wait_recv()
        state_s, state_f = os_in_stat[h], far_in_stat[h]
        peak_s, peak_m = state_s[:1], top[h][:1]
        peak_f = jnp.where(live(4), state_f[:1], FEW)
        peak = jnp.maximum(jnp.maximum(peak_s, peak_m), peak_f)
        by_s, by_m, by_f = jnp.exp2(peak_s - peak), jnp.exp2(peak_m - peak), jnp.exp2(peak_f - peak)
        mixed = acc[h]
        whole = state_s[1:2] * by_s + mixed[HD : HD + 1] * by_m + state_f[1:2] * by_f
        share = 1.0 / whole
        attended = (
            os_in[h].astype(F32) * (by_s * share)
            + mixed[:HD] * (by_m * share)
            + far_in[h].astype(F32) * (by_f * share)
        )
        ag[h, :, pl.ds(pl.multiple_of(tp * HD, HD), HD)] = jnp.transpose(attended).astype(BF16)
        for i in range(3):
            ag_copy(i, h).start()

    merge(0)
    w_own_copy.wait()
    w_sibling().wait_recv()

    @pl.loop(1, heads)
    def _(h):
        merge(h)
        project(h - 1)

    project(heads - 1)
    for i in range(parts):
        res_copy(i).wait_recv()
    table = gate_ref[...].astype(F32)
    pick = lax.broadcasted_iota(jnp.int32, table.shape, 0).astype(F32) == step
    gate = jnp.sum(jnp.where(pick, table, 0.0), axis=0, keepdims=True)
    out_ref[...] = (res[...].astype(F32) + gate * total[...]).astype(BF16)

    for copy in est_copies:
        copy.wait_send()
    for i, by in st_moves:
        st_copy(i, by).wait_send()
    for i in range(parts):
        res_copy(i).wait_send()
    w_sibling().wait_send()

    @pl.when(core == y // 2)
    def _():
        @pl.loop(0, heads)
        def _(h):
            w_across(0, h).wait_send()
            w_across(1, h).wait_send()

    def sent(h):
        for copy in (
            q_copy,
            q_forward,
            k_copy,
            v_copy,
            k_forward,
            v_forward,
            os_copy,
            os_stat_copy,
            far_copy,
            far_stat_copy,
        ):
            copy(h).wait_send()
        for i in range(3):
            w_along(i, h).wait_send()
            ag_copy(i, h).wait_send()

    each(sent)


def local(
    queries,
    key_rows,
    value_rows,
    query_gain,
    key_gain,
    out_weight,
    residual,
    gate_table,
    timesteps,
    windows,
    queue_positions,
    fresh_span,
):
    spans = lax.axis_size("tm")
    rows, width = queries.shape
    heads = width // HD
    out_cols = residual.shape[1]
    gain = (query_gain * key_gain * (HD ** (-0.5) * LOG2E)).reshape(heads, HD)
    weight = out_weight.reshape(heads, HD, out_weight.shape[1])
    chunk = pltpu.VMEM((heads, rows, HD), BF16)
    flat = pltpu.VMEM((heads, HD, rows), BF16)
    tall = pltpu.VMEM((heads, HD + 16, rows), BF16)
    stats = pltpu.VMEM((heads, 8, rows), F32)
    one = pltpu.SemaphoreType.DMA
    per_head = one((heads,))
    parts = 4
    hbm = pl.BlockSpec(memory_space=pl.ANY)
    vmem = pl.BlockSpec(memory_space=pltpu.VMEM)
    smem = pl.BlockSpec(memory_space=pltpu.SMEM)

    def run(*operands):
        def body(*refs):
            kernel(spans, *refs)

        return pl.pallas_call(
            body,
            out_shape=jax.ShapeDtypeStruct((rows, out_cols), BF16),
            in_specs=[hbm, hbm, hbm, vmem, hbm, hbm, vmem, smem, smem, smem],
            out_specs=vmem,
            scratch_shapes=[
                chunk,
                chunk,
                chunk,
                tall,
                chunk,
                chunk,
                chunk,
                chunk,
                chunk,
                tall,
                chunk,
                tall,
                pltpu.VMEM((4, 8, rows), F32),
                pltpu.VMEM((8, rows), F32),
                pltpu.VMEM((4, 8, rows), F32),
                flat,
                stats,
                flat,
                stats,
                flat,
                stats,
                flat,
                stats,
                pltpu.VMEM((heads, HD + 16, rows), F32),
                stats,
                pltpu.VMEM((heads, rows, 4 * HD), BF16),
                pltpu.VMEM((heads, 4 * HD, out_cols), BF16),
                pltpu.VMEM((rows, out_cols), BF16),
                pltpu.VMEM((rows, out_cols), F32),
                one((3, heads)),
                one,
                one((3,)),
                one((4,)),
                one((4,)),
                one((4,)),
                per_head,
                per_head,
                per_head,
                per_head,
                per_head,
                per_head,
                per_head,
                per_head,
                per_head,
                per_head,
                per_head,
                per_head,
                per_head,
                per_head,
                per_head,
                per_head,
                per_head,
                per_head,
                per_head,
                per_head,
                one((parts,)),
                one((parts,)),
                one,
                one,
                one((2, heads)),
                per_head,
                one((3, heads)),
                one((3, heads)),
                one((3, heads)),
                one((4, heads)),
            ],
            compiler_params=pltpu.CompilerParams(
                collective_id=0, has_side_effects=True, vmem_limit_bytes=56 * 2**20
            ),
            name="window_block",
        )(*operands)

    updated = run(
        queries,
        key_rows,
        value_rows,
        gain,
        weight,
        residual,
        gate_table,
        timesteps,
        windows,
        queue_positions,
    )
    return jnp.where(queue_positions[0] == 0, fresh_span, updated)


def solution(mesh):
    placed = (
        P("tm", "tp"),
        P("tm", "tp"),
        P("tm", "tp"),
        P("tp"),
        P("tp"),
        P("tp", None),
        P("tm", "tp"),
        P(None, "tp"),
        P("tm"),
        P("tm"),
        P("tm"),
        P(None, "tp"),
    )
    return jax.shard_map(
        local, mesh=mesh, in_specs=placed, out_specs=P("tm", "tp"), check_vma=False
    )
```

time: 389 us -> 205 us (0.53)
  the two profiles are of different devices: /device:TPU:1 before, /device:TPU:253 now
where the time goes in v1:
time: 205 us
  Pallas kernels  199 us (97%)
  other arithmetic  3.81 us (2%)
    pallas_call x1, Pallas kernels, run(): pl.pallas_call(body, out_shape=jax.ShapeDtypeStruct((rows, out_cols), BF1...  199 us

profile of v1, /device:TPU:253, one launch (start us, length us, event | category | flops | bytes accessed | tf_op | source)
XLA Modules:
  0.0 205.1 jit_solution(16864967882921309753)
XLA Ops:
  0.7 1.3 multiply_bitcast_fusion.refs_3_
  3.2 0.0 copy-start
  3.3 199.3 %window_block.1 = bf16[512,1280]{1,0:T(8,128)(2,1)} custom-call(bf16[512,640]{1,0:T(8,128)(2,1)} %refs_0_.1, bf16[512,640]{1,0:T(8,128)(2,1)} %refs_1_.1, bf16[512,640]{1,0:T(8,128)(2,1)} %refs_2_.1, f32[5,128]{1,0:T(8,128)} %multiply_bitcast_fusion.refs_3_, bf16[5,128,5120]{2,1,0:T(8,128)(2,1)} %bitcast.4, bf16[512,1280]{1,0:T(8,128)(2,1)} %refs_5_.1, ...), custom_call_target="tpu_custom_call" | custom-call | tf_op jit(solution)/shard_map/window_block/pallas_call | solution.py:550
  202.6 0.0 copy-done
  202.6 2.5 %broadcast_select_fusion = bf16[512,1280]{1,0:T(8,128)(2,1)} fusion(bf16[512,1280]{1,0:T(8,128)(2,1)S(1)} %copy-done, bf16[512,1280]{1,0:T(8,128)(2,1)} %window_block.1, pred[]{:T(512)} %bitcast), kind=kLoop, calls=%fused_computation | loop fusion | flops 655360 | bytes 3932161 | tf_op jit(solution)/shard_map/jit(_where)/select_n | solution.py:640
Async XLA Ops:
  3.2 199.4 %copy-start = (bf16[512,1280]{1,0:T(8,128)(2,1)S(1)}, bf16[512,1280]{1,0:T(8,128)(2,1)}, u32[]{:S(2)}) copy-start(bf16[512,1280]{1,0:T(8,128)(2,1)} %param.23) | copy-start | bytes 3932164

commit v2 on v1

--- a/solution.py
+++ b/solution.py
@@ -21,10 +21,12 @@
     q_hbm,
     k_hbm,
     v_hbm,
-    gain_ref,
+    q_gain_ref,
+    k_gain_ref,
     w_hbm,
     res_hbm,
     gate_ref,
+    fresh_hbm,
     step_ref,
     reach_ref,
     pos_ref,
@@ -58,8 +60,11 @@
     wbuf,
     res,
     total,
+    gain_buf,
+    fresh,
     load_sem,
     wload_sem,
+    fresh_sem,
     est_s,
     est_r,
     st_s,
@@ -94,6 +99,8 @@
     wy_r,
     ag_s,
     ag_r,
+    wz_s,
+    gate_sem,
 ):
     heads, rows = q_own.shape[0], q_own.shape[1]
     local = heads * HD
@@ -110,7 +117,7 @@
 
     peers = [(tm, lax.rem(tp + by, 4)) for by in (1, 2, 3)]
     across = [(tm + 8 - 16 * x_hi, (1 - lo) * 2 + c) for c in (0, 1)]
-    turn = jnp.where(z >= 4, -16, 16)
+    turn = jnp.where(z >= 4, 16, -16)
     y_next, y_prev = shifted(turn), shifted(-turn)
     turn_y = turn // 16
 
@@ -124,10 +131,19 @@
         for h in range(heads):
             load(src, dst, slot, h).start()
 
+    first, last = z == 0, z == 7
+    edge = jnp.logical_or(first, last)
+    inner = jnp.logical_not(edge)
+    opposite = [(y * 16 + (i // 4) * 8 + 7 - z, i % 4) for i in range(8)]
     barrier = pltpu.get_barrier_semaphore()
     greet = [shifted(1), shifted(-1), shifted(2), shifted(-2)] + peers + across + [y_prev]
     for other in greet:
         pl.semaphore_signal(barrier, inc=1, device_id=other, device_id_type=MESH)
+
+    @pl.when(edge)
+    def _():
+        for other in opposite:
+            pl.semaphore_signal(barrier, inc=1, device_id=other, device_id_type=MESH)
 
     w_own_copy = pltpu.make_async_copy(
         w_hbm.at[:, :, pl.ds(pl.multiple_of(tp * out_cols, HD), out_cols)],
@@ -135,35 +151,28 @@
         wload_sem,
     )
     w_own_copy.start()
+    fresh_copy = pltpu.make_async_copy(fresh_hbm, fresh, fresh_sem)
+    fresh_copy.start()
 
     ones = jnp.ones((16, rows), BF16)
     for h in range(heads):
+        both = q_gain_ref[h * HD : (h + 1) * HD] * k_gain_ref[h * HD : (h + 1) * HD]
+        gain_buf[h] = both * (HD ** (-0.5) * LOG2E)
         vt_own[h, HD : HD + 16, :] = ones
         vt1[h, HD : HD + 16, :] = ones
         vt2[h, HD : HD + 16, :] = ones
 
-    def energy_of(ref, slot, src):
+    def energy_of(ref):
         squares = jnp.zeros((rows, HD), F32)
         for h in range(heads):
-            load(src, ref, slot, h).wait()
             wide = ref[h].astype(F32)
             squares = squares + wide * wide
         return jnp.sum(jnp.transpose(squares), axis=0, keepdims=True)
 
-    energy_q = energy_of(q_own, 0, q_hbm)
-    energy_k = energy_of(k_own, 1, k_hbm)
-    line = lax.broadcasted_iota(jnp.int32, (8, rows), 0)
-    message = jnp.where(line == 0, energy_q, 0.0)
-    message = jnp.where(line == 1, energy_k, message)
-    message = jnp.where(line == 2, reach_ref[0].astype(F32) * 0.25, message)
-    message = jnp.where(line == 3, step_ref[0].astype(F32) * 0.25, message)
-    est[tp] = message
-
-    for h in range(heads):
-        load(v_hbm, v_own, 2, h).wait()
-        vt_own[h, :HD, :] = jnp.transpose(v_own[h])
-
-    pl.semaphore_wait(barrier, len(greet))
+    for src, dst, slot in loads:
+        for h in range(heads):
+            load(src, dst, slot, h).wait()
+    pl.semaphore_wait(barrier, len(greet) + len(opposite) * edge.astype(jnp.int32))
 
     def remote(src, dst, send, recv, to):
         return pltpu.make_async_remote_copy(
@@ -258,6 +267,10 @@
         slot = w_piece(y, h)
         return remote(slot, slot, wx_s.at[0, h], wx_r.at[h], across[0])
 
+    def w_outward(h, to):
+        slot = w_piece(y, h)
+        return remote(slot, slot, wz_s.at[h], wx_r.at[h], to)
+
     def w_along(k, h):
         slot = w_piece(lax.rem(y - turn_y * k + 4, 4), h)
         return remote(slot, slot, wy_s.at[k, h], wy_r.at[k, h], y_next)
@@ -269,25 +282,62 @@
     def ag_slot(h, who):
         return ag.at[h, :, pl.ds(pl.multiple_of(who * HD, HD), HD)]
 
-    def ag_copy(i, h):
-        return remote(ag_slot(h, tp), ag_slot(h, tp), ag_s.at[i, h], ag_r.at[tp, h], peers[i])
-
-    def ag_in(i, h):
-        who = lax.rem(tp + i + 1, 4)
-        return remote(ag_slot(h, who), ag_slot(h, who), ag_s.at[i, h], ag_r.at[who, h], peers[i])
+    partner = (tm, (1 - lo) * 2 + core)
+    diagonal = (1 - lo) * 2 + 1 - core
+
+    def ag_move(i, h, who, to):
+        return remote(ag_slot(h, who), ag_slot(h, who), ag_s.at[i, h], ag_r.at[who, h], to)
+
+    def ag_copies(h):
+        return [
+            ag_move(0, h, tp, partner),
+            ag_move(1, h, tp, sibling),
+            ag_move(2, h, partner[1], sibling),
+        ]
 
     def each(body):
         @pl.loop(0, heads)
         def _(h):
             body(h)
 
+    def begin_up():
+        @pl.loop(0, heads)
+        def _(h):
+            q_copy(h).start()
+
+    def begin_keys():
+        for h in range(2):
+            k_copy(h).start()
+
+    def begin_values():
+        for h in range(heads):
+            if h >= 2:
+                k_copy(h).start()
+            v_copy(h).start()
+
+    pl.when(jnp.logical_not(last))(begin_up)
+    pl.when(jnp.logical_not(first))(begin_keys)
+
+    @pl.when(jnp.logical_and(core == y // 2, inner))
+    def _():
+        @pl.loop(0, heads)
+        def _(h):
+            w_across(0, h).start()
+            w_across(1, h).start()
+
+    energy_q = energy_of(q_own)
+    energy_k = energy_of(k_own)
+    line = lax.broadcasted_iota(jnp.int32, (8, rows), 0)
+    message = jnp.where(line == 0, energy_q, 0.0)
+    message = jnp.where(line == 1, energy_k, message)
+    message = jnp.where(line == 2, reach_ref[0].astype(F32) * 0.25, message)
+    message = jnp.where(line == 3, step_ref[0].astype(F32) * 0.25, message)
+    est[tp] = message
     for copy in est_copies:
         copy.start()
-    for h in range(2):
-        q_copy(h).start()
-        k_copy(h).start()
-        v_copy(h).start()
-
+    for h in range(heads):
+        vt_own[h, :HD, :] = jnp.transpose(v_own[h])
+    pl.when(jnp.logical_not(first))(begin_values)
     for i in range(3):
         est_in(i).wait_recv()
     st_own[...] = est[0] + est[1] + est[2] + est[3]
@@ -295,27 +345,48 @@
     for i, by in st_moves:
         st_copy(i, by).start()
 
-    @pl.loop(2, heads)
-    def _(h):
-        q_copy(h).start()
-        k_copy(h).start()
-        v_copy(h).start()
-
-    @pl.when(core == y // 2)
+
+    @pl.when(edge)
     def _():
+        for other in opposite:
+            pl.semaphore_signal(gate_sem, inc=1, device_id=other, device_id_type=MESH)
+        pl.semaphore_wait(gate_sem, len(opposite))
+
+    pl.when(last)(begin_up)
+
+    @pl.when(first)
+    def _():
+        begin_keys()
+        begin_values()
+
+    w_sibling().start()
+    def begin_residual():
+        for i in range(parts // 2):
+            res_copy(i).start()
+
+    def pass_weights():
         @pl.loop(0, heads)
         def _(h):
-            w_across(0, h).start()
-            w_across(1, h).start()
-
-    w_sibling().start()
+            w_across_in(h).wait_recv()
+            w_along(0, h).start()
+
+            @pl.when(z == 1)
+            def _():
+                w_outward(h, down).start()
+
+            @pl.when(z == 6)
+            def _():
+                w_outward(h, up).start()
+
+    pl.when(z == 6)(pass_weights)
+    pl.when(z != 6)(begin_residual)
 
     def column(state, row):
         scale = lax.rsqrt(state[row : row + 1, :] / width + EPS)
         return jnp.transpose(jnp.broadcast_to(scale, (HD, rows)))
 
     def unit_q(raw, scale, h):
-        return (raw.astype(F32) * scale * gain_ref[pl.ds(h, 1), :]).astype(BF16)
+        return (raw.astype(F32) * scale * gain_buf[pl.ds(h, 1), :]).astype(BF16)
 
     def unit_k(raw, scale):
         return (raw.astype(F32) * scale).astype(BF16)
@@ -350,8 +421,11 @@
         os_stat_copy(h).start()
 
     each(self_part)
-    for i in range(parts):
+    for i in range(parts // 2, parts):
         res_copy(i).start()
+
+    pl.when(z == 6)(begin_residual)
+    pl.when(jnp.logical_and(inner, z != 6))(pass_weights)
 
     st_copy(0, 1).wait_recv()
     state_a = st_in.at[0]
@@ -396,8 +470,11 @@
         v_copy(h).wait_recv()
         v_forward(h).start()
         join(h, unit_k(k1[h], k1_scale), vt1[h], live(2))
-        w_across_in(h).wait_recv()
-        w_along(0, h).start()
+
+        @pl.when(edge)
+        def _():
+            w_across_in(h).wait_recv()
+            w_along(0, h).start()
 
     each(second_part)
 
@@ -420,11 +497,18 @@
         w_along_in(0, h).wait_recv()
         w_along(1, h).start()
 
+        @pl.when(h > 0)
+        def _():
+            w_along_in(1, h - 1).wait_recv()
+            w_along(2, h - 1).start()
+
     each(third_part)
+    w_along_in(1, heads - 1).wait_recv()
+    w_along(2, heads - 1).start()
 
     def project(h):
-        for i in range(3):
-            ag_in(i, h).wait_recv()
+        ag_move(0, h, sibling[1], sibling).wait_recv()
+        ag_move(0, h, diagonal, sibling).wait_recv()
         w_along_in(2, h).wait_recv()
 
         @pl.loop(0, out_cols // 256)
@@ -436,8 +520,6 @@
     total[...] = jnp.zeros_like(total)
 
     def merge(h):
-        w_along_in(1, h).wait_recv()
-        w_along(2, h).start()
         os_copy(h).wait_recv()
         os_stat_copy(h).wait_recv()
         far_copy(h).wait_recv()
@@ -456,25 +538,38 @@
             + far_in[h].astype(F32) * (by_f * share)
         )
         ag[h, :, pl.ds(pl.multiple_of(tp * HD, HD), HD)] = jnp.transpose(attended).astype(BF16)
-        for i in range(3):
-            ag_copy(i, h).start()
+        for copy in ag_copies(h)[:2]:
+            copy.start()
+
+    def relay(h):
+        ag_move(0, h, partner[1], partner).wait_recv()
+        ag_copies(h)[2].start()
 
     merge(0)
     w_own_copy.wait()
     w_sibling().wait_recv()
 
-    @pl.loop(1, heads)
+    merge(1)
+    relay(0)
+
+    @pl.loop(2, heads)
     def _(h):
         merge(h)
-        project(h - 1)
-
+        relay(h - 1)
+        project(h - 2)
+
+    relay(heads - 1)
+    project(heads - 2)
     project(heads - 1)
     for i in range(parts):
         res_copy(i).wait_recv()
     table = gate_ref[...].astype(F32)
     pick = lax.broadcasted_iota(jnp.int32, table.shape, 0).astype(F32) == step
     gate = jnp.sum(jnp.where(pick, table, 0.0), axis=0, keepdims=True)
-    out_ref[...] = (res[...].astype(F32) + gate * total[...]).astype(BF16)
+    fresh_copy.wait()
+    updated = (res[...].astype(F32) + gate * total[...]).astype(BF16)
+    newest = jnp.full(updated.shape, pos_ref[0], jnp.int32) == 0
+    out_ref[...] = jnp.where(newest, fresh[...], updated)
 
     for copy in est_copies:
         copy.wait_send()
@@ -484,12 +579,18 @@
         res_copy(i).wait_send()
     w_sibling().wait_send()
 
-    @pl.when(core == y // 2)
+    @pl.when(jnp.logical_and(core == y // 2, inner))
     def _():
         @pl.loop(0, heads)
         def _(h):
             w_across(0, h).wait_send()
             w_across(1, h).wait_send()
+
+    @pl.when(jnp.logical_or(z == 1, z == 6))
+    def _():
+        @pl.loop(0, heads)
+        def _(h):
+            w_outward(h, down).wait_send()
 
     def sent(h):
         for copy in (
@@ -507,7 +608,8 @@
             copy(h).wait_send()
         for i in range(3):
             w_along(i, h).wait_send()
-            ag_copy(i, h).wait_send()
+        for copy in ag_copies(h):
+            copy.wait_send()
 
     each(sent)
 
@@ -530,7 +632,6 @@
     rows, width = queries.shape
     heads = width // HD
     out_cols = residual.shape[1]
-    gain = (query_gain * key_gain * (HD ** (-0.5) * LOG2E)).reshape(heads, HD)
     weight = out_weight.reshape(heads, HD, out_weight.shape[1])
     chunk = pltpu.VMEM((heads, rows, HD), BF16)
     flat = pltpu.VMEM((heads, HD, rows), BF16)
@@ -550,7 +651,7 @@
         return pl.pallas_call(
             body,
             out_shape=jax.ShapeDtypeStruct((rows, out_cols), BF16),
-            in_specs=[hbm, hbm, hbm, vmem, hbm, hbm, vmem, smem, smem, smem],
+            in_specs=[hbm, hbm, hbm, vmem, vmem, hbm, hbm, vmem, hbm, smem, smem, smem],
             out_specs=vmem,
             scratch_shapes=[
                 chunk,
@@ -582,7 +683,10 @@
                 pltpu.VMEM((heads, 4 * HD, out_cols), BF16),
                 pltpu.VMEM((rows, out_cols), BF16),
                 pltpu.VMEM((rows, out_cols), F32),
+                pltpu.VMEM((heads, HD), F32),
+                pltpu.VMEM((rows, out_cols), BF16),
                 one((3, heads)),
+                one,
                 one,
                 one((3,)),
                 one((4,)),
@@ -618,6 +722,8 @@
                 one((3, heads)),
                 one((3, heads)),
                 one((4, heads)),
+                per_head,
+                pltpu.SemaphoreType.REGULAR,
             ],
             compiler_params=pltpu.CompilerParams(
                 collective_id=0, has_side_effects=True, vmem_limit_bytes=56 * 2**20
@@ -625,19 +731,20 @@
             name="window_block",
         )(*operands)
 
-    updated = run(
+    return run(
         queries,
         key_rows,
         value_rows,
-        gain,
+        query_gain,
+        key_gain,
         weight,
         residual,
         gate_table,
+        fresh_span,
         timesteps,
         windows,
         queue_positions,
     )
-    return jnp.where(queue_positions[0] == 0, fresh_span, updated)
 
 
 def solution(mesh):

time: 205 us -> 126 us (0.61)
  the two profiles are of different devices: /device:TPU:253 before, /device:TPU:1 now
where the time goes in v2:
time: 126 us; the launch traced here: 125 us
  Pallas kernels  121 us (96%)
  local copies, waits for them, and re-layouts  2.46 us (2%)
  between operations  1.95 us (2%)
    pallas_call x1, Pallas kernels, run(): pl.pallas_call(body, out_shape=jax.ShapeDtypeStruct((rows, out_cols), BF1...  121 us

profile of v2, /device:TPU:1, one launch (start us, length us, event | category | flops | bytes accessed | tf_op | source)
XLA Modules:
  0.0 125.5 jit_solution(15834764711880531904)
XLA Ops:
  1.9 121.1 %window_block.1 = bf16[512,1280]{1,0:T(8,128)(2,1)} custom-call(bf16[512,640]{1,0:T(8,128)(2,1)} %refs_0_.1, bf16[512,640]{1,0:T(8,128)(2,1)} %refs_1_.1, bf16[512,640]{1,0:T(8,128)(2,1)} %refs_2_.1, f32[640]{0:T(1024)} %refs_3_.1, f32[640]{0:T(1024)} %refs_4_.1, bf16[5,128,5120]{2,1,0:T(8,128)(2,1)} %bitcast.1, bf16[512,1280]{1,0:T(8,128)(2,1)} %refs_6_.1, ...), custom_call_target="tpu_custom_call" | custom-call | tf_op jit(solution)/shard_map/window_block/pallas_call | solution.py:651
  123.0 2.5 %copy.17 = bf16[512,1280]{1,0:T(8,128)(2,1)} copy(bf16[512,1280]{1,0:T(8,128)(2,1)} %window_block.1) | data formatting | bytes 2621440

commit v3 on v2

v3 whole, which is shorter than its diff:
```python
import jax
import jax.numpy as jnp
from jax import lax
from jax.experimental import pallas as pl
from jax.experimental.pallas import tpu as pltpu
from jax.sharding import PartitionSpec as P

HD = 128
WMAX = 4
EPS = 1e-06
FEW = -1e30
MANY = 1e30
LOG2E = 1.4426950408889634
MESH = pl.DeviceIdType.MESH
F32 = jnp.float32
BF16 = jnp.bfloat16


def kernel(
    spans,
    q_hbm,
    k_hbm,
    v_hbm,
    q_gain_ref,
    k_gain_ref,
    w_hbm,
    res_hbm,
    gate_ref,
    fresh_hbm,
    step_ref,
    reach_ref,
    pos_ref,
    out_ref,
    q_own,
    k_own,
    v_own,
    vt_own,
    qn,
    kn,
    qa,
    qb,
    k1,
    vt1,
    k2,
    vt2,
    est,
    st_own,
    st_in,
    os_out,
    os_stat,
    os_in,
    os_in_stat,
    far_out,
    far_stat,
    far_in,
    far_in_stat,
    acc,
    top,
    ag,
    wbuf,
    res,
    total,
    gain_buf,
    gate_buf,
    fresh,
    load_sem,
    wload_sem,
    fresh_sem,
    est_s,
    est_r,
    st_s,
    st_r,
    q_s,
    q_r,
    qf_s,
    qf_r,
    k_s,
    k_r,
    v_s,
    v_r,
    kf_s,
    kf_r,
    vf_s,
    vf_r,
    os_s,
    os_r,
    oss_s,
    oss_r,
    far_s,
    far_r,
    fars_s,
    fars_r,
    res_s,
    res_r,
    wsib_s,
    wsib_r,
    wx_s,
    wx_r,
    wy_s,
    wy_r,
    ag_s,
    ag_r,
    wz_s,
    wz_r,
    gate_sem,
):
    heads, rows = q_own.shape[0], q_own.shape[1]
    local = heads * HD
    width = 4 * local
    out_cols = out_ref.shape[1]
    strip, half, sideways = HD // 4, HD // 8, 3
    tm = lax.axis_index("tm")
    tp = lax.axis_index("tp")
    lo, core = tp // 2, tp % 2
    x_hi, y, z = (tm // 8) % 2, tm // 16, tm % 8

    def shifted(by):
        return (lax.rem(tm + by + spans, spans), tp)

    peers = [(tm, lax.rem(tp + by, 4)) for by in (1, 2, 3)]
    across = [(tm + 8 - 16 * x_hi, (1 - lo) * 2 + c) for c in (0, 1)]
    sides = [[(tm, (1 - lo) * 2 + c) for c in (0, 1)], across]
    turn = jnp.where(z >= 4, 16, -16)
    y_next, y_prev = shifted(turn), shifted(-turn)
    turn_y = turn // 16

    def load(src, dst, slot, h):
        return pltpu.make_async_copy(
            src.at[:, pl.ds(pl.multiple_of(h * HD, HD), HD)], dst.at[h], load_sem.at[slot, h]
        )

    loads = [(q_hbm, q_own, 0), (k_hbm, k_own, 1), (v_hbm, v_own, 2)]
    for src, dst, slot in loads:
        for h in range(heads):
            load(src, dst, slot, h).start()

    first, last = z == 0, z == 7
    edge = jnp.logical_or(first, last)
    inner = jnp.logical_not(edge)
    opposite = [(y * 16 + (i // 4) * 8 + 7 - z, i % 4) for i in range(8)]
    barrier = pltpu.get_barrier_semaphore()
    greet = [shifted(1), shifted(-1), shifted(2), shifted(-2)] + peers + across + [y_prev]
    for other in greet:
        pl.semaphore_signal(barrier, inc=1, device_id=other, device_id_type=MESH)

    @pl.when(edge)
    def _():
        for other in opposite:
            pl.semaphore_signal(barrier, inc=1, device_id=other, device_id_type=MESH)

    w_own_copy = pltpu.make_async_copy(
        w_hbm.at[:, :, pl.ds(pl.multiple_of(tp * out_cols, HD), out_cols)],
        wbuf.at[:, tp],
        wload_sem,
    )
    w_own_copy.start()
    fresh_copy = pltpu.make_async_copy(fresh_hbm, fresh, fresh_sem)
    fresh_copy.start()

    def energy_of(ref):
        squares = jnp.zeros((rows, HD), F32)
        for h in range(heads):
            wide = ref[h].astype(F32)
            squares = squares + wide * wide
        return jnp.sum(jnp.transpose(squares), axis=0, keepdims=True)

    for src, dst, slot in loads[:2]:
        for h in range(heads):
            load(src, dst, slot, h).wait()
    energy_q = energy_of(q_own)
    energy_k = energy_of(k_own)
    line = lax.broadcasted_iota(jnp.int32, (8, rows), 0)
    message = jnp.where(line == 0, energy_q, 0.0)
    message = jnp.where(line == 1, energy_k, message)
    message = jnp.where(line == 2, reach_ref[0].astype(F32) * 0.25, message)
    message = jnp.where(line == 3, step_ref[0].astype(F32) * 0.25, message)
    est[tp] = message
    pl.semaphore_wait(barrier, len(greet) + len(opposite) * edge.astype(jnp.int32))

    def remote(src, dst, send, recv, to):
        return pltpu.make_async_remote_copy(
            src_ref=src, dst_ref=dst, send_sem=send, recv_sem=recv, device_id=to, device_id_type=MESH
        )

    up, down = shifted(1), shifted(-1)
    est_copies = [
        remote(est.at[tp], est.at[tp], est_s.at[i], est_r.at[tp], to) for i, to in enumerate(peers)
    ]

    def est_in(i):
        who = lax.rem(tp + i + 1, 4)
        return remote(est.at[who], est.at[who], est_s.at[i], est_r.at[who], peers[i])

    def q_copy(h):
        return remote(q_own.at[h], qa.at[h], q_s.at[h], q_r.at[h], up)

    def q_forward(h):
        return remote(qa.at[h], qb.at[h], qf_s.at[h], qf_r.at[h], up)

    def k_copy(h):
        return remote(k_own.at[h], k1.at[h], k_s.at[h], k_r.at[h], down)

    def v_copy(h):
        return remote(
            vt_own.at[h, pl.ds(0, HD), :], vt1.at[h, pl.ds(0, HD), :], v_s.at[h], v_r.at[h], down
        )

    def k_forward(h):
        return remote(k1.at[h], k2.at[h], kf_s.at[h], kf_r.at[h], down)

    def v_forward(h):
        return remote(
            vt1.at[h, pl.ds(0, HD), :], vt2.at[h, pl.ds(0, HD), :], vf_s.at[h], vf_r.at[h], down
        )

    def os_copy(h):
        return remote(os_out.at[h], os_in.at[h], os_s.at[h], os_r.at[h], up)

    def os_stat_copy(h):
        return remote(os_stat.at[h], os_in_stat.at[h], oss_s.at[h], oss_r.at[h], up)

    def far_copy(h):
        return remote(far_out.at[h], far_in.at[h], far_s.at[h], far_r.at[h], down)

    def far_stat_copy(h):
        return remote(far_stat.at[h], far_in_stat.at[h], fars_s.at[h], fars_r.at[h], down)

    parts = res_s.shape[0]
    part_rows = rows // parts

    def res_copy(i):
        cut = pl.ds(i * part_rows, part_rows)
        return remote(res_hbm.at[cut], res.at[cut], res_s.at[i], res_r.at[i], up)

    def st_copy(i, by):
        return remote(st_own, st_in.at[i], st_s.at[i], st_r.at[i], shifted(by))

    sibling = (tm, lo * 2 + 1 - core)

    def w_sibling():
        return remote(
            w_hbm.at[:, :, pl.ds(pl.multiple_of(sibling[1] * out_cols, HD), out_cols)],
            wbuf.at[:, tp],
            wsib_s,
            wsib_r,
            sibling,
        )

    def piece_rows(piece):
        return pl.ds(pl.multiple_of(piece * strip, strip), strip)

    def w_rows(side):
        return pl.ds(pl.multiple_of(y * strip + side * half, half), half)

    def w_import(side, c, part, some):
        to = sides[side][c]
        these = pl.ds(0, some)
        return remote(
            w_hbm.at[
                these, w_rows(part), pl.ds(pl.multiple_of(to[1] * out_cols, HD), out_cols)
            ],
            wbuf.at[these, tp, w_rows(part), :],
            wx_s.at[side, c],
            wx_r.at[side, core],
            to,
        )

    def w_import_in(side, c, part, some):
        slot = wbuf.at[pl.ds(0, some), (1 - lo) * 2 + c, w_rows(part), :]
        return remote(slot, slot, wx_s.at[side, c], wx_r.at[side, c], sides[side][c])

    def w_exports(act):
        @pl.when(inner)
        def _():
            for side in (0, 1):
                for c in (0, 1):
                    act(w_import(side, c, side, heads))

        for side in (0, 1):

            @pl.when(jnp.logical_and(edge, core == side))
            def _():
                for c in (0, 1):
                    act(w_import(side, c, 0, sideways))

    def w_piece(piece, h):
        return wbuf.at[h, pl.ds((1 - lo) * 2, 2), piece_rows(piece), :]

    def w_outward(h, to, rows_there):
        slot = wbuf.at[h, pl.ds((1 - lo) * 2, 2), rows_there, :]
        return remote(slot, slot, wz_s.at[h], wz_r.at[h], to)

    def outward(h, to, act):
        @pl.when(h < sideways)
        def _():
            act(w_outward(h, to, w_rows(1)))

        @pl.when(h >= sideways)
        def _():
            act(w_outward(h, to, piece_rows(y)))

    def w_along(k, h):
        slot = w_piece(lax.rem(y - turn_y * k + 4, 4), h)
        return remote(slot, slot, wy_s.at[k, h], wy_r.at[k, h], y_next)

    def w_along_in(k, h):
        slot = w_piece(lax.rem(y - turn_y * (k + 1) + 8, 4), h)
        return remote(slot, slot, wy_s.at[k, h], wy_r.at[k, h], y_next)

    half_rows = rows // 2

    def ag_slot(h, who, cut):
        return ag.at[h, who, cut]

    def unit(u):
        if isinstance(u, int) and u >= heads - 1:
            return heads - 1, pl.ds((u - heads + 1) * half_rows, half_rows)
        return u, pl.ds(0, rows)

    partner = (tm, (1 - lo) * 2 + core)
    diagonal = (1 - lo) * 2 + 1 - core

    def ag_move(i, u, who, to):
        h, cut = unit(u)
        slot = ag_slot(h, who, cut)
        return remote(slot, slot, ag_s.at[i, u], ag_r.at[who, u], to)

    def ag_copies(u):
        return [
            ag_move(0, u, tp, partner),
            ag_move(1, u, tp, sibling),
            ag_move(2, u, partner[1], sibling),
        ]

    def each(body):
        @pl.loop(0, heads)
        def _(h):
            body(h)

    def begin_up(some, end):
        @pl.loop(some, end)
        def _(h):
            q_copy(h).start()

    def begin_keys():
        for h in range(early):
            k_copy(h).start()

    def begin_values():
        for h in range(early):
            v_copy(h).start()

    def begin_rest():
        @pl.loop(early, heads)
        def _(h):
            k_copy(h).start()
            v_copy(h).start()

    early = 2
    for copy in est_copies:
        copy.start()
    pl.when(jnp.logical_not(first))(begin_keys)

    @pl.when(jnp.logical_not(last))
    def _():
        begin_up(0, early)

    w_exports(lambda copy: copy.start())

    ones = jnp.ones((16, rows), BF16)
    for h in range(heads):
        load(v_hbm, v_own, 2, h).wait()
        vt_own[h, :HD, :] = jnp.transpose(v_own[h])
        vt_own[h, HD : HD + 16, :] = ones
        if h == early - 1:
            pl.when(jnp.logical_not(first))(begin_values)

    for i in range(3):
        est_in(i).wait_recv()
    st_own[...] = est[0] + est[1] + est[2] + est[3]
    st_moves = [(0, 1), (1, 2), (2, -1), (3, -2)]
    for i, by in st_moves:
        st_copy(i, by).start()

    @pl.when(jnp.logical_not(last))
    def _():
        begin_up(early, heads)

    pl.when(jnp.logical_not(first))(begin_rest)
    for h in range(heads):
        both = q_gain_ref[h * HD : (h + 1) * HD] * k_gain_ref[h * HD : (h + 1) * HD]
        gain_buf[h] = both * (HD ** (-0.5) * LOG2E)
        vt1[h, HD : HD + 16, :] = ones
        vt2[h, HD : HD + 16, :] = ones

    def pass_weights():
        for side in (0, 1):
            for c in (0, 1):
                w_import_in(side, c, side, heads).wait_recv()

        @pl.loop(0, heads)
        def _(h):
            w_along(0, h).start()

            @pl.when(z == 1)
            def _():
                outward(h, down, lambda copy: copy.start())

            @pl.when(z == 6)
            def _():
                outward(h, up, lambda copy: copy.start())

    pl.when(inner)(pass_weights)

    @pl.when(edge)
    def _():
        for side in (0, 1):
            w_import_in(side, side, 0, sideways).wait_recv()
        for other in opposite:
            pl.semaphore_signal(gate_sem, inc=1, device_id=other, device_id_type=MESH)
        pl.semaphore_wait(gate_sem, len(opposite))

    @pl.when(last)
    def _():
        begin_up(0, heads)

    @pl.when(first)
    def _():
        begin_keys()
        begin_values()
        begin_rest()

    w_sibling().start()
    def begin_residual():
        for i in range(parts // 2):
            res_copy(i).start()

    pl.when(z != 6)(begin_residual)

    def column(state, row):
        scale = lax.rsqrt(state[row : row + 1, :] / width + EPS)
        return jnp.transpose(jnp.broadcast_to(scale, (HD, rows)))

    def unit_q(raw, scale, h):
        return (raw.astype(F32) * scale * gain_buf[pl.ds(h, 1), :]).astype(BF16)

    def unit_k(raw, scale):
        return (raw.astype(F32) * scale).astype(BF16)

    def scores_of(keys, queries):
        return lax.dot_general(
            keys, queries, (((1,), (1,)), ((), ())), preferred_element_type=F32
        )

    def alone(keys, queries, values):
        scores = scores_of(keys, queries)
        peak = jnp.max(scores, axis=0, keepdims=True)
        weight = jnp.exp2(scores - peak).astype(BF16)
        return jnp.dot(values, weight, preferred_element_type=F32), peak

    fold = rows // HD

    def pair(first, second):
        return jnp.concatenate(
            [one[:, i * HD : (i + 1) * HD] for one in (first, second) for i in range(fold)], axis=0
        )

    def unpair(packed):
        first = jnp.concatenate([packed[i : i + 1] for i in range(fold)], axis=1)
        second = jnp.concatenate([packed[fold + i : fold + i + 1] for i in range(fold)], axis=1)
        return first, second

    q_scale = column(st_own, 0)
    k_scale = column(st_own, 1)

    def self_part(h):
        q_copy(h).wait_recv()
        q_forward(h).start()
        kn[h] = unit_k(k_own[h], k_scale)
        mixed, peak = alone(kn[h], unit_q(q_own[h], q_scale, h), vt_own[h])
        os_out[h] = mixed[:HD].astype(BF16)
        os_stat[h] = pair(peak, mixed[HD : HD + 1])
        os_copy(h).start()
        os_stat_copy(h).start()

    each(self_part)
    pl.when(z == 6)(begin_residual)
    for i in range(parts // 2, parts):
        res_copy(i).start()

    st_copy(0, 1).wait_recv()
    state_a = st_in.at[0]
    reach = state_a[2:3, :]
    step = state_a[3:4, :1]
    place = lax.rem(pos_ref[0] + spans - 1, spans)

    def live(distance):
        inside = (place + distance <= spans - 1).astype(F32)
        return jnp.logical_and(reach >= distance, inside > 0.5)

    qa_scale = column(state_a, 0)

    def near_part(h):
        qn[h] = unit_q(qa[h], qa_scale, h)
        scores = scores_of(kn[h], qn[h])
        allowed = live(1)
        peak = jnp.max(scores, axis=0, keepdims=True)
        weight = jnp.exp2(scores - jnp.where(allowed, peak, MANY)).astype(BF16)
        acc[h] = jnp.dot(vt_own[h], weight, preferred_element_type=F32)
        top[h] = jnp.broadcast_to(jnp.where(allowed, peak, FEW), (8, rows))

    each(near_part)

    def join(h, keys, values, allowed):
        scores = scores_of(keys, qn[h])
        before = top[h][:1]
        peak = jnp.where(allowed, jnp.max(scores, axis=0, keepdims=True), FEW)
        after = jnp.maximum(before, peak)
        weight = jnp.exp2(scores - jnp.where(allowed, after, MANY)).astype(BF16)
        acc[h] = acc[h] * jnp.exp2(before - after) + jnp.dot(
            values, weight, preferred_element_type=F32
        )
        top[h] = jnp.broadcast_to(after, (8, rows))

    st_copy(2, -1).wait_recv()
    k1_scale = column(st_in.at[2], 1)

    def second_part(h):
        k_copy(h).wait_recv()
        k_forward(h).start()
        v_copy(h).wait_recv()
        v_forward(h).start()
        join(h, unit_k(k1[h], k1_scale), vt1[h], live(2))

        @pl.when(edge)
        def _():
            outward(h, up, lambda copy: copy.wait_recv())
            w_along(0, h).start()

    each(second_part)

    st_copy(1, 2).wait_recv()
    st_copy(3, -2).wait_recv()
    qb_scale = column(st_in.at[1], 0)
    k2_scale = column(st_in.at[3], 1)

    def third_part(h):
        q_forward(h).wait_recv()
        k_forward(h).wait_recv()
        v_forward(h).wait_recv()
        keys = unit_k(k2[h], k2_scale)
        mixed, peak = alone(keys, unit_q(qb[h], qb_scale, h), vt2[h])
        far_out[h] = mixed[:HD].astype(BF16)
        far_stat[h] = pair(peak, mixed[HD : HD + 1])
        far_copy(h).start()
        far_stat_copy(h).start()
        join(h, keys, vt2[h], live(3))
        w_along_in(0, h).wait_recv()
        w_along(1, h).start()

        @pl.when(h > 0)
        def _():
            w_along_in(1, h - 1).wait_recv()
            w_along(2, h - 1).start()

    each(third_part)
    w_along_in(1, heads - 1).wait_recv()
    w_along(2, heads - 1).start()

    def tiles(body):
        @pl.loop(0, out_cols // 256)
        def _(j):
            body(pl.ds(pl.multiple_of(j * 256, 256), 256))

    def product(h, cut):
        left = jnp.concatenate([ag[h, i] for i in range(4)], axis=1)
        return jnp.dot(left, wbuf[h, :, :, cut].reshape(4 * HD, 256), preferred_element_type=F32)

    def project(h):
        ag_move(0, h, sibling[1], sibling).wait_recv()
        ag_move(0, h, diagonal, sibling).wait_recv()
        w_along_in(2, h).wait_recv()

        def body(cut):
            total[:, cut] = total[:, cut] + product(h, cut)

        tiles(body)

    total[...] = jnp.zeros_like(total)

    def arrived(h):
        os_copy(h).wait_recv()
        os_stat_copy(h).wait_recv()
        far_copy(h).wait_recv()
        far_stat_copy(h).wait_recv()

    def merge(u):
        h, _ = unit(u)
        cut = slice(0, rows)
        if isinstance(u, int) and u >= heads - 1:
            cut = slice((u - heads + 1) * half_rows, (u - heads + 2) * half_rows)
        peak_s, sum_s = (one[:, cut] for one in unpair(os_in_stat[h]))
        peak_f, sum_f = (one[:, cut] for one in unpair(far_in_stat[h]))
        peak_m = top[h, :1, cut]
        peak_f = jnp.where(live(4)[:, cut], peak_f, FEW)
        peak = jnp.maximum(jnp.maximum(peak_s, peak_m), peak_f)
        by_s, by_m, by_f = jnp.exp2(peak_s - peak), jnp.exp2(peak_m - peak), jnp.exp2(peak_f - peak)
        mixed = acc[h, :, cut]
        whole = sum_s * by_s + mixed[HD : HD + 1] * by_m + sum_f * by_f
        share = 1.0 / whole
        attended = (
            os_in[h, :, cut].astype(F32) * (by_s * share)
            + mixed[:HD] * (by_m * share)
            + far_in[h, :, cut].astype(F32) * (by_f * share)
        )
        ag[h, tp, cut] = jnp.transpose(attended).astype(BF16)
        for copy in ag_copies(u)[:2]:
            copy.start()

    def relay(u):
        ag_move(0, u, partner[1], partner).wait_recv()
        ag_copies(u)[2].start()

    w_own_copy.wait()
    w_sibling().wait_recv()
    final = heads - 1
    for h in range(final):
        arrived(h)
        merge(h)
        if h >= 2:
            relay(h - 2)
        if h >= 3:
            project(h - 3)
    arrived(final)
    merge(final)
    merge(final + 1)
    for h in range(final - 2, final):
        relay(h)
        project(h - 1)
    for i in range(parts):
        res_copy(i).wait_recv()
    fresh_copy.wait()
    table = gate_ref[...].astype(F32)
    pick = lax.broadcasted_iota(jnp.int32, table.shape, 0).astype(F32) == step
    gate_buf[...] = jnp.sum(jnp.where(pick, table, 0.0), axis=0, keepdims=True)
    relay(final)
    relay(final + 1)
    project(final - 1)
    w_along_in(2, final).wait_recv()

    for u in (final, final + 1):
        ag_move(0, u, sibling[1], sibling).wait_recv()
        ag_move(0, u, diagonal, sibling).wait_recv()
        part = slice((u - final) * half_rows, (u - final + 1) * half_rows)

        def finish(cut, part=part):
            right = wbuf[final, :, :, cut].reshape(4 * HD, 256)
            left = jnp.concatenate([ag[final, i, part] for i in range(4)], axis=1)
            last_term = jnp.dot(left, right, preferred_element_type=F32)
            projected = total[part, cut] + last_term
            updated = (res[part, cut].astype(F32) + gate_buf[:, cut] * projected).astype(BF16)
            newest = jnp.full(updated.shape, pos_ref[0], jnp.int32) == 0
            out_ref[part, cut] = jnp.where(newest, fresh[part, cut], updated)

        tiles(finish)

    for copy in est_copies:
        copy.wait_send()
    for i, by in st_moves:
        st_copy(i, by).wait_send()
    for i in range(parts):
        res_copy(i).wait_send()
    w_sibling().wait_send()

    w_exports(lambda copy: copy.wait_send())

    @pl.when(jnp.logical_or(z == 1, z == 6))
    def _():
        @pl.loop(0, heads)
        def _(h):
            outward(h, down, lambda copy: copy.wait_send())

    def sent(h):
        for copy in (
            q_copy,
            q_forward,
            k_copy,
            v_copy,
            k_forward,
            v_forward,
            os_copy,
            os_stat_copy,
            far_copy,
            far_stat_copy,
        ):
            copy(h).wait_send()
        for i in range(3):
            w_along(i, h).wait_send()

    each(sent)
    for u in range(heads + 1):
        for copy in ag_copies(u):
            copy.wait_send()


def local(
    queries,
    key_rows,
    value_rows,
    query_gain,
    key_gain,
    out_weight,
    residual,
    gate_table,
    timesteps,
    windows,
    queue_positions,
    fresh_span,
):
    spans = lax.axis_size("tm")
    rows, width = queries.shape
    heads = width // HD
    out_cols = residual.shape[1]
    weight = out_weight.reshape(heads, HD, out_weight.shape[1])
    chunk = pltpu.VMEM((heads, rows, HD), BF16)
    flat = pltpu.VMEM((heads, HD, rows), BF16)
    tall = pltpu.VMEM((heads, HD + 16, rows), BF16)
    stats = pltpu.VMEM((heads, 8, rows), F32)
    packed = pltpu.VMEM((heads, 2 * (rows // HD), HD), F32)
    one = pltpu.SemaphoreType.DMA
    per_head = one((heads,))
    parts = 4
    hbm = pl.BlockSpec(memory_space=pl.ANY)
    vmem = pl.BlockSpec(memory_space=pltpu.VMEM)
    smem = pl.BlockSpec(memory_space=pltpu.SMEM)

    def run(*operands):
        def body(*refs):
            kernel(spans, *refs)

        return pl.pallas_call(
            body,
            out_shape=jax.ShapeDtypeStruct((rows, out_cols), BF16),
            in_specs=[hbm, hbm, hbm, vmem, vmem, hbm, hbm, vmem, hbm, smem, smem, smem],
            out_specs=vmem,
            scratch_shapes=[
                chunk,
                chunk,
                chunk,
                tall,
                chunk,
                chunk,
                chunk,
                chunk,
                chunk,
                tall,
                chunk,
                tall,
                pltpu.VMEM((4, 8, rows), F32),
                pltpu.VMEM((8, rows), F32),
                pltpu.VMEM((4, 8, rows), F32),
                flat,
                packed,
                flat,
                packed,
                flat,
                packed,
                flat,
                packed,
                pltpu.VMEM((heads, HD + 16, rows), F32),
                stats,
                pltpu.VMEM((heads, 4, rows, HD), BF16),
                pltpu.VMEM((heads, 4, HD, out_cols), BF16),
                pltpu.VMEM((rows, out_cols), BF16),
                pltpu.VMEM((rows, out_cols), F32),
                pltpu.VMEM((heads, HD), F32),
                pltpu.VMEM((1, out_cols), F32),
                pltpu.VMEM((rows, out_cols), BF16),
                one((3, heads)),
                one,
                one,
                one((3,)),
                one((4,)),
                one((4,)),
                one((4,)),
                per_head,
                per_head,
                per_head,
                per_head,
                per_head,
                per_head,
                per_head,
                per_head,
                per_head,
                per_head,
                per_head,
                per_head,
                per_head,
                per_head,
                per_head,
                per_head,
                per_head,
                per_head,
                per_head,
                per_head,
                one((parts,)),
                one((parts,)),
                one,
                one,
                one((2, 2)),
                one((2, 2)),
                one((3, heads)),
                one((3, heads)),
                one((3, heads + 1)),
                one((4, heads + 1)),
                per_head,
                per_head,
                pltpu.SemaphoreType.REGULAR,
            ],
            compiler_params=pltpu.CompilerParams(
                collective_id=0, has_side_effects=True, vmem_limit_bytes=56 * 2**20
            ),
            name="window_block",
        )(*operands)

    return run(
        queries,
        key_rows,
        value_rows,
        query_gain,
        key_gain,
        weight,
        residual,
        gate_table,
        fresh_span,
        timesteps,
        windows,
        queue_positions,
    )


def solution(mesh):
    placed = (
        P("tm", "tp"),
        P("tm", "tp"),
        P("tm", "tp"),
        P("tp"),
        P("tp"),
        P("tp", None),
        P("tm", "tp"),
        P(None, "tp"),
        P("tm"),
        P("tm"),
        P("tm"),
        P(None, "tp"),
    )
    return jax.shard_map(
        local, mesh=mesh, in_specs=placed, out_specs=P("tm", "tp"), check_vma=False
    )
```

time: 126 us -> 120 us (0.952)
  Pallas kernels: 121 us -> 116 us
    pallas_call x1, Pallas kernels: 121 us -> 116 us  [run(): pl.pallas_call(body, out_shape=jax.ShapeDtypeStruct((rows, out_cols), BF1...]
where the time goes in v3:
time: 120 us
  Pallas kernels  116 us (97%)
  local copies, waits for them, and re-layouts  2.46 us (2%)
  between operations  1.95 us (2%)
    pallas_call x1, Pallas kernels, run(): pl.pallas_call(body, out_shape=jax.ShapeDtypeStruct((rows, out_cols), BF1...  116 us
    unnamed x1, local copies, waits for them, and re-layouts  2.46 us

profile of v3, /device:TPU:1, one launch (start us, length us, event | category | flops | bytes accessed | tf_op | source)
XLA Modules:
  0.0 120.3 jit_solution(3471933418990278538)
XLA Ops:
  1.9 115.9 %window_block.1 = bf16[512,1280]{1,0:T(8,128)(2,1)} custom-call(bf16[512,640]{1,0:T(8,128)(2,1)} %refs_0_.1, bf16[512,640]{1,0:T(8,128)(2,1)} %refs_1_.1, bf16[512,640]{1,0:T(8,128)(2,1)} %refs_2_.1, f32[640]{0:T(1024)} %refs_3_.1, f32[640]{0:T(1024)} %refs_4_.1, bf16[5,128,5120]{2,1,0:T(8,128)(2,1)} %bitcast.1, bf16[512,1280]{1,0:T(8,128)(2,1)} %refs_6_.1, ...), custom_call_target="tpu_custom_call" | custom-call | tf_op jit(solution)/shard_map/window_block/pallas_call | solution.py:741
  117.9 2.5 %copy.17 = bf16[512,1280]{1,0:T(8,128)(2,1)} copy(bf16[512,1280]{1,0:T(8,128)(2,1)} %window_block.1) | data formatting | bytes 2621440

commit v4 on v3

--- a/solution.py
+++ b/solution.py
@@ -740,7 +740,7 @@
 
         return pl.pallas_call(
             body,
-            out_shape=jax.ShapeDtypeStruct((rows, out_cols), BF16),
+            out_shape=pltpu.VMEM((rows, out_cols), BF16),
             in_specs=[hbm, hbm, hbm, vmem, vmem, hbm, hbm, vmem, hbm, smem, smem, smem],
             out_specs=vmem,
             scratch_shapes=[

time: 120 us -> 118 us (0.983)
  local copies, waits for them, and re-layouts: 2.46 us -> 1.06 us
    unnamed x1, local copies, waits for them, and re-layouts: 2.46 us -> 1.06 us
where the time goes in v4:
time: 118 us
  Pallas kernels  115 us (97%)
  between operations  1.95 us (2%)
    pallas_call x1, Pallas kernels, run(): pl.pallas_call(body, out_shape=pltpu.VMEM((rows, out_cols), BF16), in_spe...  115 us

profile of v4, /device:TPU:1, one launch (start us, length us, event | category | flops | bytes accessed | tf_op | source)
XLA Modules:
  0.0 117.9 jit_solution(17643715101118597980)
XLA Ops:
  1.9 114.9 %window_block.1 = bf16[512,1280]{1,0:T(8,128)(2,1)S(1)} custom-call(bf16[512,640]{1,0:T(8,128)(2,1)} %refs_0_.1, bf16[512,640]{1,0:T(8,128)(2,1)} %refs_1_.1, bf16[512,640]{1,0:T(8,128)(2,1)} %refs_2_.1, f32[640]{0:T(1024)} %refs_3_.1, f32[640]{0:T(1024)} %refs_4_.1, bf16[5,128,5120]{2,1,0:T(8,128)(2,1)} %bitcast.1, bf16[512,1280]{1,0:T(8,128)(2,1)} %refs_6_.1, ...), custom_call_target="tpu_custom_call" | custom-call | tf_op jit(solution)/shard_map/window_block/pallas_call | solution.py:741
  116.8 1.1 copy.14

commit v5 on v4

--- a/solution.py
+++ b/solution.py
@@ -643,27 +643,6 @@
     table = gate_ref[...].astype(F32)
     pick = lax.broadcasted_iota(jnp.int32, table.shape, 0).astype(F32) == step
     gate_buf[...] = jnp.sum(jnp.where(pick, table, 0.0), axis=0, keepdims=True)
-    relay(final)
-    relay(final + 1)
-    project(final - 1)
-    w_along_in(2, final).wait_recv()
-
-    for u in (final, final + 1):
-        ag_move(0, u, sibling[1], sibling).wait_recv()
-        ag_move(0, u, diagonal, sibling).wait_recv()
-        part = slice((u - final) * half_rows, (u - final + 1) * half_rows)
-
-        def finish(cut, part=part):
-            right = wbuf[final, :, :, cut].reshape(4 * HD, 256)
-            left = jnp.concatenate([ag[final, i, part] for i in range(4)], axis=1)
-            last_term = jnp.dot(left, right, preferred_element_type=F32)
-            projected = total[part, cut] + last_term
-            updated = (res[part, cut].astype(F32) + gate_buf[:, cut] * projected).astype(BF16)
-            newest = jnp.full(updated.shape, pos_ref[0], jnp.int32) == 0
-            out_ref[part, cut] = jnp.where(newest, fresh[part, cut], updated)
-
-        tiles(finish)
-
     for copy in est_copies:
         copy.wait_send()
     for i, by in st_moves:
@@ -698,6 +677,28 @@
             w_along(i, h).wait_send()
 
     each(sent)
+
+    relay(final)
+    relay(final + 1)
+    project(final - 1)
+    w_along_in(2, final).wait_recv()
+
+    for u in (final, final + 1):
+        ag_move(0, u, sibling[1], sibling).wait_recv()
+        ag_move(0, u, diagonal, sibling).wait_recv()
+        part = slice((u - final) * half_rows, (u - final + 1) * half_rows)
+
+        def finish(cut, part=part):
+            right = wbuf[final, :, :, cut].reshape(4 * HD, 256)
+            left = jnp.concatenate([ag[final, i, part] for i in range(4)], axis=1)
+            last_term = jnp.dot(left, right, preferred_element_type=F32)
+            projected = total[part, cut] + last_term
+            updated = (res[part, cut].astype(F32) + gate_buf[:, cut] * projected).astype(BF16)
+            newest = jnp.full(updated.shape, pos_ref[0], jnp.int32) == 0
+            out_ref[part, cut] = jnp.where(newest, fresh[part, cut], updated)
+
+        tiles(finish)
+
     for u in range(heads + 1):
         for copy in ag_copies(u):
             copy.wait_send()

time: 118 us -> 118 us (level)
  no operation moved by 1% of the time
where the time goes in v5:
time: 118 us
  Pallas kernels  115 us (97%)
  between operations  1.95 us (2%)
    pallas_call x1, Pallas kernels, run(): pl.pallas_call(body, out_shape=pltpu.VMEM((rows, out_cols), BF16), in_spe...  115 us

profile of v5, /device:TPU:1, one launch (start us, length us, event | category | flops | bytes accessed | tf_op | source)
XLA Modules:
  0.0 117.9 jit_solution(15538960652076112827)
XLA Ops:
  1.9 114.9 %window_block.1 = bf16[512,1280]{1,0:T(8,128)(2,1)S(1)} custom-call(bf16[512,640]{1,0:T(8,128)(2,1)} %refs_0_.1, bf16[512,640]{1,0:T(8,128)(2,1)} %refs_1_.1, bf16[512,640]{1,0:T(8,128)(2,1)} %refs_2_.1, f32[640]{0:T(1024)} %refs_3_.1, f32[640]{0:T(1024)} %refs_4_.1, bf16[5,128,5120]{2,1,0:T(8,128)(2,1)} %bitcast.1, bf16[512,1280]{1,0:T(8,128)(2,1)} %refs_6_.1, ...), custom_call_target="tpu_custom_call" | custom-call | tf_op jit(solution)/shard_map/window_block/pallas_call | solution.py:742
  116.8 1.1 copy.14

commit v6 on v4

--- a/solution.py
+++ b/solution.py
@@ -367,6 +367,21 @@
 
     w_exports(lambda copy: copy.start())
 
+    for i in range(3):
+        est_in(i).wait_recv()
+
+    @pl.when(edge)
+    def _():
+        for side in (0, 1):
+            w_import_in(side, side, 0, sideways).wait_recv()
+        for other in opposite:
+            pl.semaphore_signal(gate_sem, inc=1, device_id=other, device_id_type=MESH)
+
+    st_own[...] = est[0] + est[1] + est[2] + est[3]
+    st_moves = [(0, 1), (1, 2), (2, -1), (3, -2)]
+    for i, by in st_moves:
+        st_copy(i, by).start()
+
     ones = jnp.ones((16, rows), BF16)
     for h in range(heads):
         load(v_hbm, v_own, 2, h).wait()
@@ -375,13 +390,6 @@
         if h == early - 1:
             pl.when(jnp.logical_not(first))(begin_values)
 
-    for i in range(3):
-        est_in(i).wait_recv()
-    st_own[...] = est[0] + est[1] + est[2] + est[3]
-    st_moves = [(0, 1), (1, 2), (2, -1), (3, -2)]
-    for i, by in st_moves:
-        st_copy(i, by).start()
-
     @pl.when(jnp.logical_not(last))
     def _():
         begin_up(early, heads)
@@ -414,10 +422,6 @@
 
     @pl.when(edge)
     def _():
-        for side in (0, 1):
-            w_import_in(side, side, 0, sideways).wait_recv()
-        for other in opposite:
-            pl.semaphore_signal(gate_sem, inc=1, device_id=other, device_id_type=MESH)
         pl.semaphore_wait(gate_sem, len(opposite))
 
     @pl.when(last)

time: 118 us -> 118 us (level)
  no operation moved by 1% of the time
where the time goes in v6:
time: 118 us
  Pallas kernels  115 us (97%)
  between operations  1.95 us (2%)
    pallas_call x1, Pallas kernels, run(): pl.pallas_call(body, out_shape=pltpu.VMEM((rows, out_cols), BF16), in_spe...  115 us

profile of v6, /device:TPU:1, one launch (start us, length us, event | category | flops | bytes accessed | tf_op | source)
XLA Modules:
  0.0 117.8 jit_solution(13949544678042395150)
XLA Ops:
  1.9 114.8 %window_block.1 = bf16[512,1280]{1,0:T(8,128)(2,1)S(1)} custom-call(bf16[512,640]{1,0:T(8,128)(2,1)} %refs_0_.1, bf16[512,640]{1,0:T(8,128)(2,1)} %refs_1_.1, bf16[512,640]{1,0:T(8,128)(2,1)} %refs_2_.1, f32[640]{0:T(1024)} %refs_3_.1, f32[640]{0:T(1024)} %refs_4_.1, bf16[5,128,5120]{2,1,0:T(8,128)(2,1)} %bitcast.1, bf16[512,1280]{1,0:T(8,128)(2,1)} %refs_6_.1, ...), custom_call_target="tpu_custom_call" | custom-call | tf_op jit(solution)/shard_map/window_block/pallas_call | solution.py:745
  116.8 1.1 copy.14
